TPU v7x, 32 devices: a whole 2x2x4 slice. The times are simulated.
32 devices in a mesh: dp: 8 (over y, x, core), seq: 4 (over z).
Axes of the slice: x: 2, y: 2, z: 4, core: 2. Of those that a mesh axis runs over, the one named last changes fastest.
Arguments:
- inputs: bfloat16 [16, 2048, 640], P('dp', 'seq'), may hold values from -6 to 6
- cotangent: bfloat16 [16, 2048, 640], P('dp', 'seq'), may hold values from -6 to 6
- w_query: bfloat16 [640, 1024], P('seq', 'dp'), may hold values from -0.25 to 0.25
- w_key: bfloat16 [640, 256], P('seq', 'dp'), may hold values from -0.25 to 0.25
- w_value: bfloat16 [640, 256], P('seq', 'dp'), may hold values from -0.25 to 0.25
- w_out: bfloat16 [1024, 640], P('seq', 'dp'), may hold values from -0.1875 to 0.1875
- w_gate: bfloat16 [640, 2048], P('seq', 'dp'), may hold values from -0.25 to 0.25
- w_up: bfloat16 [640, 2048], P('seq', 'dp'), may hold values from -0.25 to 0.25
- w_down: bfloat16 [2048, 640], P('seq', 'dp'), may hold values from -0.125 to 0.125
- gains: bfloat16 [48, 64], P('seq', 'dp'), may hold values from -0.5 to 0.5
Outputs:
- outputs: bfloat16 [16, 2048, 640], P('dp', 'seq')
- grad_inputs: bfloat16 [16, 2048, 640], P('dp', 'seq')
- grad_query: float32 [640, 1024], P('seq', 'dp')
- grad_key: float32 [640, 256], P('seq', 'dp')
- grad_value: float32 [640, 256], P('seq', 'dp')
- grad_out: float32 [1024, 640], P('seq', 'dp')
- grad_gate: float32 [640, 2048], P('seq', 'dp')
- grad_up: float32 [640, 2048], P('seq', 'dp')
- grad_down: float32 [2048, 640], P('seq', 'dp')
- grad_gains: float32 [48, 64], P('seq', 'dp')
All inputs are finite; a program needn't handle non-finite values.
Results may differ from a plain program's by a relative error of at most 0.022.
Values may be sent and summed in bfloat16 or wider, within the bound.
A program may use at most 192 MiB of HBM per device.

v0:
```python
import jax
import jax.numpy as jnp
from jax import lax
from jax.sharding import PartitionSpec as P

D = 640
HEADS = 4
HD = 256
WINDOW = 512
MB = 2


EPS = 1e-06
MASKED = -1e30


def shifted(value, axis, steps):
    count = lax.axis_size(axis)
    first, last = (max(0, -steps), min(count, count - steps))
    return lax.ppermute(value, axis, [(source, source + steps) for source in range(first, last)])


def rms_norm(vector, scale_gain):
    factor = lax.rsqrt(jnp.mean(vector * vector, axis=-1, keepdims=True) + EPS)
    return vector * factor * (1.0 + scale_gain)


def angles(positions, head_width):
    ladder = jnp.arange(head_width // 2).astype(jnp.float32) * 2.0
    inverse = 10000.0 ** (-ladder / head_width)
    return positions[:, None] * inverse[None, :]


def rotate(vector, angle_table):
    middle_at = vector.shape[-1] // 2
    leading = vector[..., :middle_at]
    trailing = vector[..., middle_at:]
    cosine = jnp.cos(angle_table)
    sine_of = jnp.sin(angle_table)
    return jnp.concatenate(
        [leading * cosine - trailing * sine_of, trailing * cosine + leading * sine_of], axis=-1
    )


def gated_unit(gate_val, up_val):
    return jax.nn.gelu(gate_val, approximate=True) * up_val


def product(left_side, right_side):
    flat_left = left_side.reshape(-1, left_side.shape[-1])
    result = jnp.dot(flat_left, right_side, preferred_element_type=jnp.float32)
    return result.reshape(left_side.shape[:-1] + (right_side.shape[-1],))


def outer_sum(left_side, right_side):
    flat_left = left_side.reshape(-1, left_side.shape[-1])
    flat_right = right_side.reshape(-1, right_side.shape[-1])
    return lax.dot_general(
        flat_left, flat_right, (((0,), (0,)), ((), ())), preferred_element_type=jnp.float32
    )


def back_product(gradient, weight):
    flat_grad = gradient.reshape(-1, gradient.shape[-1])
    result = lax.dot_general(
        flat_grad, weight, (((1,), (1,)), ((), ())), preferred_element_type=jnp.float32
    )
    return result.reshape(gradient.shape[:-1] + (weight.shape[0],))


def local_grads(function, primals, cotangent_in):
    return jax.vjp(function, *primals)[1](cotangent_in)


def split_gains(full_gains):
    flat_gains = full_gains.astype(jnp.float32).reshape(-1)
    return (
        flat_gains[0:D],
        flat_gains[D : 2 * D],
        flat_gains[2 * D : 3 * D],
        flat_gains[3 * D : 4 * D],
        flat_gains[4 * D : 4 * D + HD],
        flat_gains[4 * D + HD : 4 * D + 2 * HD],
    )


def masked_scores(queries, key_block, query_pos, key_pos):
    scores = jnp.einsum(
        "sqhd,skd->shqk", queries, key_block, preferred_element_type=jnp.float32
    ) * HD ** (-0.5)
    distance = query_pos[:, None] - key_pos[None, :]
    allowed = (distance >= 0) & (distance < WINDOW) & (key_pos[None, :] >= 0)
    return jnp.where(allowed[None, None], scores, MASKED)


def local(inputs, cotangent, w_query, w_key, w_value, w_out, w_gate, w_up, w_down, gains):
    groups = inputs.shape[0]
    stretch_len = inputs.shape[1]
    per_batch = groups // MB
    heads_width = HEADS * HD
    seq_index = lax.axis_index("seq")
    query_pos = seq_index * stretch_len + jnp.arange(stretch_len, dtype=jnp.int32)
    angle_table = angles(query_pos.astype(jnp.float32), HD)
    reach_stretches = WINDOW // stretch_len
    key_span = WINDOW + stretch_len

    def query_path(q_lin, g_query):
        return rotate(rms_norm(q_lin, g_query), angle_table[:, None, :])

    def key_path(k_lin, g_key):
        return rotate(rms_norm(k_lin, g_key), angle_table)

    def collect():
        wide_parts = (
            lax.all_gather(w_query, "dp", axis=1, tiled=True),
            lax.all_gather(w_key, "dp", axis=1, tiled=True),
            lax.all_gather(w_value, "dp", axis=1, tiled=True),
            lax.all_gather(w_out, "dp", axis=1, tiled=True),
            lax.all_gather(w_gate, "dp", axis=1, tiled=True),
            lax.all_gather(w_up, "dp", axis=1, tiled=True),
            lax.all_gather(w_down, "dp", axis=1, tiled=True),
            lax.all_gather(gains, "dp", axis=1, tiled=True),
        )
        part_query, part_key, part_value, part_out, part_gate, part_up, part_down, part_gains = (
            wide_parts
        )
        return (
            lax.all_gather(part_query, "seq", axis=0, tiled=True),
            lax.all_gather(part_key, "seq", axis=0, tiled=True),
            lax.all_gather(part_value, "seq", axis=0, tiled=True),
            lax.all_gather(part_out, "seq", axis=0, tiled=True),
            lax.all_gather(part_gate, "seq", axis=0, tiled=True),
            lax.all_gather(part_up, "seq", axis=0, tiled=True),
            lax.all_gather(part_down, "seq", axis=0, tiled=True),
            lax.all_gather(part_gains, "seq", axis=0, tiled=True),
        )

    def fetch_weights():
        return collect()

    key_pos = (
        seq_index * stretch_len
        - reach_stretches * stretch_len
        + jnp.arange(key_span, dtype=jnp.int32)
    )
    out_blocks = []
    kept_list = []
    for micro_batch in range(MB):
        (
            forward_full_query,
            forward_full_key,
            forward_full_value,
            forward_full_out,
            forward_full_gate,
            forward_full_up,
            forward_full_down,
            forward_full_gains,
        ) = fetch_weights()
        (
            forward_g_attn_in,
            forward_g_attn_out,
            forward_g_ffw_in,
            forward_g_ffw_out,
            forward_g_query,
            forward_g_key,
        ) = split_gains(forward_full_gains)
        forward_first_row = micro_batch * per_batch
        forward_resid = inputs[forward_first_row : forward_first_row + per_batch].astype(
            jnp.float32
        )
        forward_normed = rms_norm(forward_resid, forward_g_attn_in).astype(jnp.bfloat16)
        forward_q_lin = product(forward_normed, forward_full_query).reshape(
            per_batch, stretch_len, HEADS, HD
        )
        forward_k_lin = product(forward_normed, forward_full_key)
        v_lin = product(forward_normed, forward_full_value)
        forward_queries = query_path(forward_q_lin, forward_g_query).astype(jnp.bfloat16)
        forward_keys_b = key_path(forward_k_lin, forward_g_key).astype(jnp.bfloat16)
        forward_values_b = v_lin.astype(jnp.bfloat16)
        key_parts = [forward_keys_b]
        value_parts = [forward_values_b]
        for fetch_offset in range(1, reach_stretches + 1):
            moved_keys, moved_values = shifted(
                (forward_keys_b, forward_values_b), "seq", fetch_offset
            )
            key_parts.insert(0, moved_keys)
            value_parts.insert(0, moved_values)
        forward_key_block = jnp.concatenate(key_parts, axis=1)
        forward_value_block = jnp.concatenate(value_parts, axis=1)
        forward_scores = masked_scores(forward_queries, forward_key_block, query_pos, key_pos)
        row_max = jnp.max(forward_scores, axis=-1, keepdims=True)
        exponent = jnp.exp(forward_scores - row_max)
        row_sum = jnp.sum(exponent, axis=-1, keepdims=True)
        attn_probs = (exponent / row_sum).astype(jnp.bfloat16)
        forward_log_sum = row_max + jnp.log(row_sum)
        forward_mixed_heads = jnp.einsum(
            "shqk,skd->sqhd", attn_probs, forward_value_block, preferred_element_type=jnp.float32
        )
        forward_mixed_heads = forward_mixed_heads.reshape(
            per_batch, stretch_len, heads_width
        ).astype(jnp.bfloat16)
        forward_attended = product(forward_mixed_heads, forward_full_out)
        forward_middle = forward_resid + rms_norm(forward_attended, forward_g_attn_out)
        forward_ffw_in = rms_norm(forward_middle, forward_g_ffw_in).astype(jnp.bfloat16)
        forward_gate_val = product(forward_ffw_in, forward_full_gate)
        forward_up_val = product(forward_ffw_in, forward_full_up)
        forward_hidden = gated_unit(forward_gate_val, forward_up_val).astype(jnp.bfloat16)
        forward_down_val = product(forward_hidden, forward_full_down)
        result = forward_middle + rms_norm(forward_down_val, forward_g_ffw_out)
        forward_kept_values = (
            forward_resid,
            forward_normed,
            forward_q_lin,
            forward_k_lin,
            forward_queries,
            forward_key_block,
            forward_value_block,
            forward_log_sum,
            forward_mixed_heads,
            forward_attended,
            forward_middle,
            forward_ffw_in,
            forward_gate_val,
            forward_up_val,
            forward_hidden,
            forward_down_val,
        )
        result, kept_values = (result.astype(jnp.bfloat16), forward_kept_values)
        out_blocks.append(result)
        kept_list.append(kept_values)
    grad_blocks = [None] * MB
    totals = None
    gains_shape = None
    for micro_batch in reversed(range(MB)):
        weights = fetch_weights()
        gains_shape = weights[7].shape
        backward_kept_values = kept_list[micro_batch]
        full_query, full_key, full_value, full_out, full_gate, full_up, full_down, full_gains = (
            weights
        )
        g_attn_in, g_attn_out, g_ffw_in, g_ffw_out, backward_g_query, backward_g_key = split_gains(
            full_gains
        )
        (
            resid,
            normed,
            backward_q_lin,
            backward_k_lin,
            queries,
            key_block,
            value_block,
            log_sum,
            mixed_heads,
            attended,
            middle,
            ffw_in,
            gate_val,
            up_val,
            hidden,
            down_val,
        ) = backward_kept_values
        backward_first_row = micro_batch * per_batch
        backward_grad_out = cotangent[backward_first_row : backward_first_row + per_batch].astype(
            jnp.float32
        )
        d_down, d_g_ffw_out = local_grads(rms_norm, (down_val, g_ffw_out), backward_grad_out)
        d_down = d_down.astype(jnp.bfloat16)
        term_down = outer_sum(hidden, d_down)
        d_hidden = back_product(d_down, full_down)
        d_gate, d_up = local_grads(gated_unit, (gate_val, up_val), d_hidden)
        d_gate = d_gate.astype(jnp.bfloat16)
        d_up = d_up.astype(jnp.bfloat16)
        term_gate = outer_sum(ffw_in, d_gate)
        term_up = outer_sum(ffw_in, d_up)
        d_ffw_in = back_product(d_gate, full_gate) + back_product(d_up, full_up)
        d_middle, d_g_ffw_in = local_grads(rms_norm, (middle, g_ffw_in), d_ffw_in)
        d_middle = backward_grad_out + d_middle
        d_attended, d_g_attn_out = local_grads(rms_norm, (attended, g_attn_out), d_middle)
        d_attended = d_attended.astype(jnp.bfloat16)
        term_out = outer_sum(mixed_heads, d_attended)
        d_mixed = (
            back_product(d_attended, full_out)
            .astype(jnp.bfloat16)
            .reshape(per_batch, stretch_len, HEADS, HD)
        )
        scores = masked_scores(queries, key_block, query_pos, key_pos)
        full_probs = jnp.exp(scores - log_sum)
        d_probs = jnp.einsum(
            "sqhd,skd->shqk", d_mixed, value_block, preferred_element_type=jnp.float32
        )
        d_scores = full_probs * (d_probs - jnp.sum(full_probs * d_probs, axis=-1, keepdims=True))
        d_scores = d_scores.astype(jnp.bfloat16)
        d_value_block = jnp.einsum(
            "shqk,sqhd->skd",
            full_probs.astype(jnp.bfloat16),
            d_mixed,
            preferred_element_type=jnp.float32,
        )
        d_key_block = jnp.einsum(
            "shqk,sqhd->skd", d_scores, queries, preferred_element_type=jnp.float32
        ) * HD ** (-0.5)
        d_queries = jnp.einsum(
            "shqk,skd->sqhd", d_scores, key_block, preferred_element_type=jnp.float32
        ) * HD ** (-0.5)
        own_keys = d_key_block[:, reach_stretches * stretch_len :]
        own_values = d_value_block[:, reach_stretches * stretch_len :]
        for offset in range(1, reach_stretches + 1):
            first_row = (reach_stretches - offset) * stretch_len
            back_keys, back_values = (
                shifted(
                    d_key_block[:, first_row : first_row + stretch_len].astype(jnp.bfloat16),
                    "seq",
                    -offset,
                ).astype(jnp.float32),
                shifted(
                    d_value_block[:, first_row : first_row + stretch_len].astype(jnp.bfloat16),
                    "seq",
                    -offset,
                ).astype(jnp.float32),
            )
            own_keys = own_keys + back_keys
            own_values = own_values + back_values
        d_values = own_values
        d_q_lin, d_g_query = local_grads(query_path, (backward_q_lin, backward_g_query), d_queries)
        d_k_lin, d_g_key = local_grads(key_path, (backward_k_lin, backward_g_key), own_keys)
        d_q_lin = d_q_lin.reshape(per_batch, stretch_len, heads_width).astype(jnp.bfloat16)
        d_k_lin = d_k_lin.astype(jnp.bfloat16)
        d_values = d_values.astype(jnp.bfloat16)
        term_query = outer_sum(normed, d_q_lin)
        term_key = outer_sum(normed, d_k_lin)
        term_value = outer_sum(normed, d_values)
        d_normed = (
            back_product(d_q_lin, full_query)
            + back_product(d_k_lin, full_key)
            + back_product(d_values, full_value)
        )
        d_resid, d_g_attn_in = local_grads(rms_norm, (resid, g_attn_in), d_normed)
        d_inputs = (d_middle + d_resid).astype(jnp.bfloat16)
        gain_terms = jnp.concatenate(
            [d_g_attn_in, d_g_attn_out, d_g_ffw_in, d_g_ffw_out, d_g_query, d_g_key]
        )
        d_inputs, new_terms = (
            d_inputs,
            (term_query, term_key, term_value, term_out, term_gate, term_up, term_down, gain_terms),
        )
        grad_blocks[micro_batch] = d_inputs
        if totals is None:
            totals = new_terms
        else:
            totals = tuple((earlier + later for earlier, later in zip(totals, new_terms)))
    sum_query, sum_key, sum_value, sum_out, sum_gate, sum_up, sum_down, sum_gains = totals
    sum_gains = sum_gains.reshape(gains_shape)
    row_parts = (
        lax.psum_scatter(
            sum_query.astype(jnp.bfloat16), "seq", scatter_dimension=0, tiled=True
        ).astype(jnp.float32),
        lax.psum_scatter(
            sum_key.astype(jnp.bfloat16), "seq", scatter_dimension=0, tiled=True
        ).astype(jnp.float32),
        lax.psum_scatter(
            sum_value.astype(jnp.bfloat16), "seq", scatter_dimension=0, tiled=True
        ).astype(jnp.float32),
        lax.psum_scatter(
            sum_out.astype(jnp.bfloat16), "seq", scatter_dimension=0, tiled=True
        ).astype(jnp.float32),
        lax.psum_scatter(
            sum_gate.astype(jnp.bfloat16), "seq", scatter_dimension=0, tiled=True
        ).astype(jnp.float32),
        lax.psum_scatter(
            sum_up.astype(jnp.bfloat16), "seq", scatter_dimension=0, tiled=True
        ).astype(jnp.float32),
        lax.psum_scatter(
            sum_down.astype(jnp.bfloat16), "seq", scatter_dimension=0, tiled=True
        ).astype(jnp.float32),
        lax.psum_scatter(
            sum_gains.astype(jnp.bfloat16), "seq", scatter_dimension=0, tiled=True
        ).astype(jnp.float32),
    )
    rows_query, rows_key, rows_value, rows_out, rows_gate, rows_up, rows_down, rows_gains = (
        row_parts
    )
    final_parts = (
        lax.psum_scatter(
            rows_query.astype(jnp.bfloat16), "dp", scatter_dimension=1, tiled=True
        ).astype(jnp.float32),
        lax.psum_scatter(
            rows_key.astype(jnp.bfloat16), "dp", scatter_dimension=1, tiled=True
        ).astype(jnp.float32),
        lax.psum_scatter(
            rows_value.astype(jnp.bfloat16), "dp", scatter_dimension=1, tiled=True
        ).astype(jnp.float32),
        lax.psum_scatter(
            rows_out.astype(jnp.bfloat16), "dp", scatter_dimension=1, tiled=True
        ).astype(jnp.float32),
        lax.psum_scatter(
            rows_gate.astype(jnp.bfloat16), "dp", scatter_dimension=1, tiled=True
        ).astype(jnp.float32),
        lax.psum_scatter(
            rows_up.astype(jnp.bfloat16), "dp", scatter_dimension=1, tiled=True
        ).astype(jnp.float32),
        lax.psum_scatter(
            rows_down.astype(jnp.bfloat16), "dp", scatter_dimension=1, tiled=True
        ).astype(jnp.float32),
        lax.psum_scatter(
            rows_gains.astype(jnp.bfloat16), "dp", scatter_dimension=1, tiled=True
        ).astype(jnp.float32),
    )
    grad_query, grad_key, grad_value, grad_out, grad_gate, grad_up, grad_down, grad_gains = (
        final_parts
    )
    outputs = jnp.concatenate(out_blocks, axis=0)
    grad_inputs = jnp.concatenate(grad_blocks, axis=0)
    return (
        outputs,
        grad_inputs,
        grad_query,
        grad_key,
        grad_value,
        grad_out,
        grad_gate,
        grad_up,
        grad_down,
        grad_gains,
    )


def solution(mesh):
    in_specs = (
        P("dp", "seq", None),
        P("dp", "seq", None),
        P("seq", "dp"),
        P("seq", "dp"),
        P("seq", "dp"),
        P("seq", "dp"),
        P("seq", "dp"),
        P("seq", "dp"),
        P("seq", "dp"),
        P("seq", "dp"),
    )
    out_specs = (
        P("dp", "seq", None),
        P("dp", "seq", None),
        P("seq", "dp"),
        P("seq", "dp"),
        P("seq", "dp"),
        P("seq", "dp"),
        P("seq", "dp"),
        P("seq", "dp"),
        P("seq", "dp"),
        P("seq", "dp"),
    )
    return jax.shard_map(local, mesh=mesh, in_specs=in_specs, out_specs=out_specs, check_vma=False)
```

profile of v0, /device:TPU:0, one launch (start us, length us, event | category | flops | bytes accessed | tf_op | source)
XLA Modules:
  0.0 893.1 jit_solution(10948074404849529103)
XLA Ops:
  7.3 12.9 %all_gather.38 = bf16[160,1024]{1,0:T(8,128)(2,1)} all-gather(bf16[160,128]{1,0:T(8,128)(2,1)} %param.12), channel_id=1, replica_groups=mesh['dp'=8,'seq'=4] {'dp'}, dimensions={1}, use_global_device_ids=true | all-gather | bytes 368640 | tf_op jit(solution)/shard_map/all_gather | solution.py:115
  20.2 10.3 %all_gather.40 = bf16[256,640]{0,1:T(8,128)(2,1)} all-gather(bf16[256,80]{0,1:T(8,128)(2,1)} %param.15), channel_id=1, replica_groups=mesh['dp'=8,'seq'=4] {'dp'}, dimensions={1}, use_global_device_ids=true | all-gather | bytes 368640 | tf_op jit(solution)/shard_map/all_gather | solution.py:118
  30.6 14.0 %all_gather.42 = bf16[160,2048]{1,0:T(8,128)(2,1)} all-gather(bf16[160,256]{1,0:T(8,128)(2,1)} %param.16), channel_id=1, replica_groups=mesh['dp'=8,'seq'=4] {'dp'}, dimensions={1}, use_global_device_ids=true | all-gather | bytes 737280 | tf_op jit(solution)/shard_map/all_gather | solution.py:119
  44.6 12.9 %all_gather.44 = bf16[160,2048]{1,0:T(8,128)(2,1)} all-gather(bf16[160,256]{1,0:T(8,128)(2,1)S(1)} %copy-done.88), channel_id=1, replica_groups=mesh['dp'=8,'seq'=4] {'dp'}, dimensions={1}, use_global_device_ids=true | all-gather | bytes 737280 | tf_op jit(solution)/shard_map/all_gather | solution.py:120
  57.7 8.3 all_gather.32
  66.0 13.6 %all-gather = bf16[4,12,64]{2,1,0:T(8,128)(2,1)S(1)} all-gather(bf16[1,12,64]{2,1,0:T(8,128)(2,1)S(1)} %copy.153), channel_id=1, replica_groups=mesh['dp'=8,'seq'=4] {'seq'}, dimensions={0}, use_global_device_ids=true | all-gather | bytes 7680 | tf_op jit(solution)/shard_map/all_gather | solution.py:135
  79.7 8.9 all_gather.36
  88.8 16.8 %all_gather.37 = bf16[640,256]{1,0:T(8,128)(2,1)S(1)} all-gather(bf16[160,256]{1,0:T(8,128)(2,1)S(1)} %copy.155), channel_id=1, replica_groups=mesh['dp'=8,'seq'=4] {'seq'}, dimensions={0}, use_global_device_ids=true | all-gather | bytes 409600 | tf_op jit(solution)/shard_map/all_gather | solution.py:129
  113.9 8.3 all_gather.34
  122.4 23.0 %all_gather.35 = bf16[640,256]{1,0:T(8,128)(2,1)S(1)} all-gather(bf16[160,256]{1,0:T(8,128)(2,1)S(1)} %copy.154), channel_id=1, replica_groups=mesh['dp'=8,'seq'=4] {'seq'}, dimensions={0}, use_global_device_ids=true | all-gather | bytes 409600 | tf_op jit(solution)/shard_map/all_gather | solution.py:130
  154.5 4.9 collective-permute-start
  159.4 10.2 %all_gather.46 = bf16[512,640]{0,1:T(8,128)(2,1)} all-gather(bf16[512,80]{0,1:T(8,128)(2,1)S(1)} %copy-done.89), channel_id=1, replica_groups=mesh['dp'=8,'seq'=4] {'dp'}, dimensions={1}, use_global_device_ids=true | all-gather | bytes 737280 | tf_op jit(solution)/shard_map/all_gather | solution.py:121
  214.7 8.7 multiply_reduce_fusion.10
  225.6 5.6 fusion.212
  231.2 6.6 multiply_convert_fusion.2
  237.7 31.1 %all-gather.15.cloned.1.call-done = bf16[2048,640]{0,1:T(8,128)(2,1)} async-done(((bf16[512,640]{0,1:T(8,128)(2,1)}), bf16[2048,640]{0,1:T(8,128)(2,1)}) %all-gather.15.cloned.1.call-update) | async-done | bytes 2621456 | tf_op jit(solution)/shard_map/all_gather | solution.py:134
  338.4 6.0 collective-permute-done.4
  347.9 6.6 collective-permute-done.5
  414.3 15.5 %reduce-scatter.34.cloned.1.call-done = bf16[256,640]{1,0:T(8,128)(2,1)} async-done(((bf16[1024,640]{1,0:T(8,128)(2,1)}), bf16[256,640]{1,0:T(8,128)(2,1)}) %reduce-scatter.34.cloned.1.call-update) | async-done | bytes 327696 | tf_op jit(solution)/shard_map/reduce_scatter | solution.py:363
  438.8 23.3 %reduce-scatter.28.cloned.1.call-done = bf16[160,1024]{1,0:T(8,128)(2,1)} async-done(((bf16[640,1024]{1,0:T(8,128)(2,1)}), bf16[160,1024]{1,0:T(8,128)(2,1)}) %reduce-scatter.28.cloned.1.call-update) | async-done | bytes 327696 | tf_op jit(solution)/shard_map/reduce_scatter | solution.py:354
  467.5 47.7 %reduce-scatter.44.cloned.1.call-done = bf16[512,640]{1,0:T(8,128)(2,1)} async-done(((bf16[2048,640]{1,0:T(8,128)(2,1)}), bf16[512,640]{1,0:T(8,128)(2,1)}) %reduce-scatter.44.cloned.1.call-update) | async-done | bytes 655376 | tf_op jit(solution)/shard_map/reduce_scatter | solution.py:372
  521.5 47.9 %reduce-scatter.40.cloned.1.call-done = bf16[160,2048]{1,0:T(8,128)(2,1)} async-done(((bf16[640,2048]{1,0:T(8,128)(2,1)}), bf16[160,2048]{1,0:T(8,128)(2,1)}) %reduce-scatter.40.cloned.1.call-update) | async-done | bytes 655376 | tf_op jit(solution)/shard_map/reduce_scatter | solution.py:369
  569.7 12.3 %fusion = bf16[16,64]{1,0:T(8,128)(2,1)S(1)} fusion(bf16[48,64]{1,0:T(8,128)(2,1)S(1)} %convert_element_type.383), kind=kCustom, calls=%all-reduce-scatter | all-reduce-scatter fusion | flops 4097 | bytes 8704
  583.8 39.6 %reduce-scatter.36.cloned.1.call-done = bf16[160,2048]{1,0:T(8,128)(2,1)} async-done(((bf16[640,2048]{1,0:T(8,128)(2,1)}), bf16[160,2048]{1,0:T(8,128)(2,1)}) %reduce-scatter.36.cloned.1.call-update) | async-done | bytes 655376 | tf_op jit(solution)/shard_map/reduce_scatter | solution.py:366
  627.7 13.5 %all-reduce.9 = bf16[12,64]{1,0:T(8,128)(2,1)S(1)} all-reduce(bf16[12,64]{1,0:T(8,128)(2,1)S(1)} %constant_dynamic-slice_fusion), channel_id=17, replica_groups=mesh['dp'=8,'seq'=4] {'dp'}, use_global_device_ids=true, to_apply=%region_57.58.clone | all-reduce | flops 768 | bytes 3072
  641.9 18.1 %reduce-scatter.50.cloned.1.call-done = bf16[32,160]{1,0:T(8,128)(2,1)} async-done(((bf16[256,160]{1,0:T(8,128)(2,1)}), bf16[32,160]{1,0:T(8,128)(2,1)}) %reduce-scatter.50.cloned.1.call-update) | async-done | bytes 10256
  661.5 35.6 %reduce-scatter.48.cloned.1.call-done = bf16[32,160]{1,0:T(8,128)(2,1)} async-done(((bf16[256,160]{1,0:T(8,128)(2,1)}), bf16[32,160]{1,0:T(8,128)(2,1)}) %reduce-scatter.48.cloned.1.call-update) | async-done | bytes 10256
  698.6 35.2 %reduce-scatter.52.cloned.1.call-done = bf16[80,256]{1,0:T(8,128)(2,1)} async-done(((bf16[640,256]{1,0:T(8,128)(2,1)}), bf16[80,256]{1,0:T(8,128)(2,1)}) %reduce-scatter.52.cloned.1.call-update) | async-done | bytes 40976
  735.4 35.4 %reduce-scatter.46.cloned.1.call-done = bf16[128,160]{1,0:T(8,128)(2,1)} async-done(((bf16[1024,160]{1,0:T(8,128)(2,1)}), bf16[128,160]{1,0:T(8,128)(2,1)}) %reduce-scatter.46.cloned.1.call-update) | async-done | bytes 40976
  772.5 36.3 %reduce-scatter.54.cloned.1.call-done = bf16[80,512]{1,0:T(8,128)(2,1)} async-done(((bf16[640,512]{1,0:T(8,128)(2,1)}), bf16[80,512]{1,0:T(8,128)(2,1)}) %reduce-scatter.54.cloned.1.call-update) | async-done | bytes 81936
  810.5 36.1 %reduce-scatter.42.cloned.1.call-done = bf16[160,256]{1,0:T(8,128)(2,1)} async-done(((bf16[160,2048]{1,0:T(8,128)(2,1)}), bf16[160,256]{1,0:T(8,128)(2,1)}) %reduce-scatter.42.cloned.1.call-update) | async-done | bytes 81936 | tf_op jit(solution)/shard_map/reduce_scatter | solution.py:398
  848.2 36.4 %reduce-scatter.38.cloned.1.call-done = bf16[160,256]{1,0:T(8,128)(2,1)} async-done(((bf16[160,2048]{1,0:T(8,128)(2,1)}), bf16[160,256]{1,0:T(8,128)(2,1)}) %reduce-scatter.38.cloned.1.call-update) | async-done | bytes 81936 | tf_op jit(solution)/shard_map/reduce_scatter | solution.py:395
  (556 shorter events, 233.5 us)
Async XLA Ops:
  7.2 168.2 %all-gather.7.cloned.1.call-start = ((), (), s32[]{:S(2)}) async-start(), calls=%async_computation.14 | async-start | bytes 1638400 | tf_op jit(solution)/shard_map/all_gather | solution.py:128
  20.1 190.5 %all-gather.9.cloned.1.call-start = ((), (), s32[]{:S(2)}) async-start(), calls=%async_computation.15 | async-start | bytes 1638400 | tf_op jit(solution)/shard_map/all_gather | solution.py:131
  30.5 195.1 %all-gather.11.cloned.1.call-start = ((), (), s32[]{:S(2)}) async-start(), calls=%async_computation.16 | async-start | bytes 3276800 | tf_op jit(solution)/shard_map/all_gather | solution.py:132
  44.6 186.6 %all-gather.13.cloned.1.call-start = ((), (), s32[]{:S(2)}) async-start(), calls=%async_computation.17 | async-start | bytes 3276800 | tf_op jit(solution)/shard_map/all_gather | solution.py:133
  57.6 211.2 %all-gather.15.cloned.1.call-start = ((), (), s32[]{:S(2)}) async-start(), calls=%async_computation.18 | async-start | bytes 3276800 | tf_op jit(solution)/shard_map/all_gather | solution.py:134
  79.7 100.3 %copy-start.82 = (f32[640]{0:T(1024)}, f32[640]{0:T(1024)S(1)}, u32[]{:S(2)}) copy-start(f32[640]{0:T(1024)S(1)} %add.443) | copy-start | bytes 7684
  110.3 82.1 %collective-permute-start.3 = (bf16[1,512,256]{1,2,0:T(8,128)(2,1)}, bf16[1,512,256]{1,2,0:T(8,128)(2,1)}, u32[]{:S(2)}, u32[]{:S(2)}) collective-permute-start(bf16[1,512,256]{1,2,0:T(8,128)(2,1)} %pad_maximum_fusion.9), channel_id=1, source_target_pairs={{0,1},{1,2},{2,3},{4,5},{5,6},{6,7},{8,9},{9,10},{10,11},{12,13},{... | collective-permute-start | bytes 786440 | tf_op jit(solution)/shard_map/ppermute | solution.py:20
  146.5 50.5 %collective-permute-start.2 = (bf16[1,512,256]{2,1,0:T(8,128)(2,1)}, bf16[1,512,256]{2,1,0:T(8,128)(2,1)}, u32[]{:S(2)}, u32[]{:S(2)}) collective-permute-start(bf16[1,512,256]{2,1,0:T(8,128)(2,1)} %fusion.100), channel_id=1, source_target_pairs={{0,1},{1,2},{2,3},{4,5},{5,6},{6,7},{8,9},{9,10},{10,11},{12,13},{... | collective-permute-start | bytes 786440 | tf_op jit(solution)/shard_map/ppermute | solution.py:20
  151.2 50.6 %collective-permute-start.1 = (bf16[1,512,256]{1,2,0:T(8,128)(2,1)}, bf16[1,512,256]{1,2,0:T(8,128)(2,1)}, u32[]{:S(2)}, u32[]{:S(2)}) collective-permute-start(bf16[1,512,256]{1,2,0:T(8,128)(2,1)} %pad_maximum_fusion.8), channel_id=1, source_target_pairs={{0,1},{1,2},{2,3},{4,5},{5,6},{6,7},{8,9},{9,10},{10,11},{12,13},{... | collective-permute-start | bytes 786440 | tf_op jit(solution)/shard_map/ppermute | solution.py:20
  154.5 51.4 %collective-permute-start = (bf16[1,512,256]{2,1,0:T(8,128)(2,1)}, bf16[1,512,256]{2,1,0:T(8,128)(2,1)}, u32[]{:S(2)}, u32[]{:S(2)}) collective-permute-start(bf16[1,512,256]{2,1,0:T(8,128)(2,1)} %fusion.99), channel_id=1, source_target_pairs={{0,1},{1,2},{2,3},{4,5},{5,6},{6,7},{8,9},{9,10},{10,11},{12,13},{... | collective-permute-start | bytes 786440 | tf_op jit(solution)/shard_map/ppermute | solution.py:20
  169.6 238.7 %reduce-scatter.32.cloned.1.call-start = ((), (), s32[]{:S(2)}) async-start(), calls=%async_computation.21 | async-start | bytes 409600 | tf_op jit(solution)/shard_map/reduce_scatter | solution.py:360
  323.0 15.3 %collective-permute-start.6 = (bf16[1,512,256]{1,2,0:T(8,128)(2,1)S(1)}, bf16[1,512,256]{1,2,0:T(8,128)(2,1)S(1)}, u32[]{:S(2)}, u32[]{:S(2)}) collective-permute-start(bf16[1,512,256]{1,2,0:T(8,128)(2,1)S(1)} %slice.246), channel_id=1, source_target_pairs={{1,0},{2,1},{3,2},{5,4},{6,5},{7,6},{9,8},{10,9},{11,10},{13,12},{... | collective-permute-start | bytes 786440 | tf_op jit(solution)/shard_map/ppermute | solution.py:20
  332.6 11.7 %collective-permute-start.4 = (bf16[1,512,256]{1,2,0:T(8,128)(2,1)S(1)}, bf16[1,512,256]{1,2,0:T(8,128)(2,1)S(1)}, u32[]{:S(2)}, u32[]{:S(2)}) collective-permute-start(bf16[1,512,256]{1,2,0:T(8,128)(2,1)S(1)} %slice.248), channel_id=1, source_target_pairs={{1,0},{2,1},{3,2},{5,4},{6,5},{7,6},{9,8},{10,9},{11,10},{13,12},{... | collective-permute-start | bytes 786440 | tf_op jit(solution)/shard_map/ppermute | solution.py:20
  335.5 19.5 %collective-permute-start.7 = (bf16[1,512,256]{2,1,0:T(8,128)(2,1)S(1)}, bf16[1,512,256]{2,1,0:T(8,128)(2,1)S(1)}, u32[]{:S(2)}, u32[]{:S(2)}) collective-permute-start(bf16[1,512,256]{2,1,0:T(8,128)(2,1)S(1)} %slice.245), channel_id=1, source_target_pairs={{1,0},{2,1},{3,2},{5,4},{6,5},{7,6},{9,8},{10,9},{11,10},{13,12},{... | collective-permute-start | bytes 786440 | tf_op jit(solution)/shard_map/ppermute | solution.py:20
  336.9 17.6 %collective-permute-start.5 = (bf16[1,512,256]{2,1,0:T(8,128)(2,1)S(1)}, bf16[1,512,256]{2,1,0:T(8,128)(2,1)S(1)}, u32[]{:S(2)}, u32[]{:S(2)}) collective-permute-start(bf16[1,512,256]{2,1,0:T(8,128)(2,1)S(1)} %slice.247), channel_id=1, source_target_pairs={{1,0},{2,1},{3,2},{5,4},{6,5},{7,6},{9,8},{10,9},{11,10},{13,12},{... | collective-permute-start | bytes 786440 | tf_op jit(solution)/shard_map/ppermute | solution.py:20
  357.2 53.0 %reduce-scatter.30.cloned.1.call-start = ((), (), s32[]{:S(2)}) async-start(), calls=%async_computation.20 | async-start | bytes 409600 | tf_op jit(solution)/shard_map/reduce_scatter | solution.py:357
  361.7 68.0 %reduce-scatter.34.cloned.1.call-start = ((), (), s32[]{:S(2)}) async-start(), calls=%async_computation.22 | async-start | bytes 1638400 | tf_op jit(solution)/shard_map/reduce_scatter | solution.py:363
  366.1 96.0 %reduce-scatter.28.cloned.1.call-start = ((), (), s32[]{:S(2)}) async-start(), calls=%async_computation.19 | async-start | bytes 1638400 | tf_op jit(solution)/shard_map/reduce_scatter | solution.py:354
  388.0 127.2 %reduce-scatter.44.cloned.1.call-start = ((), (), s32[]{:S(2)}) async-start(), calls=%async_computation.27 | async-start | bytes 3276800 | tf_op jit(solution)/shard_map/reduce_scatter | solution.py:372
  395.1 174.2 %reduce-scatter.40.cloned.1.call-start = ((), (), s32[]{:S(2)}) async-start(), calls=%async_computation.25 | async-start | bytes 3276800 | tf_op jit(solution)/shard_map/reduce_scatter | solution.py:369
  401.8 221.6 %reduce-scatter.36.cloned.1.call-start = ((), (), s32[]{:S(2)}) async-start(), calls=%async_computation.23 | async-start | bytes 3276800 | tf_op jit(solution)/shard_map/reduce_scatter | solution.py:366
  408.3 251.7 %reduce-scatter.50.cloned.1.call-start = ((), (), s32[]{:S(2)}) async-start(), calls=%async_computation.30 | async-start | bytes 147456
  410.1 287.0 %reduce-scatter.48.cloned.1.call-start = ((), (), s32[]{:S(2)}) async-start(), calls=%async_computation.29 | async-start | bytes 147456
  411.8 322.0 %reduce-scatter.52.cloned.1.call-start = ((), (), s32[]{:S(2)}) async-start(), calls=%async_computation.31 | async-start | bytes 368640
  431.7 339.2 %reduce-scatter.46.cloned.1.call-start = ((), (), s32[]{:S(2)}) async-start(), calls=%async_computation.28 | async-start | bytes 589824
  464.1 344.6 %reduce-scatter.54.cloned.1.call-start = ((), (), s32[]{:S(2)}) async-start(), calls=%async_computation.32 | async-start | bytes 737280
  517.4 329.2 %reduce-scatter.42.cloned.1.call-start = ((), (), s32[]{:S(2)}) async-start(), calls=%async_computation.26 | async-start | bytes 737280 | tf_op jit(solution)/shard_map/reduce_scatter | solution.py:398
  519.5 103.9 %copy-start.114 = (f32[512]{0:T(512)S(1)}, f32[512]{0:T(512)}, u32[]{:S(2)}) copy-start(f32[512]{0:T(512)} %copy-done.113) | copy-start | bytes 6148
  519.5 103.9 %copy-start.116 = (f32[512]{0:T(512)S(1)}, f32[512]{0:T(512)}, u32[]{:S(2)}) copy-start(f32[512]{0:T(512)} %copy-done.115) | copy-start | bytes 6148
  521.4 102.1 %copy-start.9 = (f32[1,512,640]{2,1,0:T(8,128)S(1)}, f32[1,512,640]{2,1,0:T(8,128)}, u32[]{:S(2)}) copy-start(f32[1,512,640]{2,1,0:T(8,128)} %copy-done.8) | copy-start | bytes 3932164
  569.4 315.2 %reduce-scatter.38.cloned.1.call-start = ((), (), s32[]{:S(2)}) async-start(), calls=%async_computation.24 | async-start | bytes 737280 | tf_op jit(solution)/shard_map/reduce_scatter | solution.py:395
  582.0 45.5 %collective-permute-start.8 = (bf16[12,64]{1,0:T(8,128)(2,1)S(1)}, bf16[12,64]{1,0:T(8,128)(2,1)S(1)}, u32[]{:S(2)}, u32[]{:S(2)}) collective-permute-start(bf16[12,64]{1,0:T(8,128)(2,1)S(1)} %slice.154), channel_id=1, source_target_pairs={{0,1},{1,2},{2,3},{4,5},{5,6},{6,7},{8,9},{9,10},{10,11},{12,13},{... | collective-permute-start | bytes 4616
  (157 other events, 1928.0 us)
Sparse Core Ops, SparseCore 0:
  20.3 32.9 all-gather.6
  54.9 32.6 all-gather.8
  89.1 67.6 all-gather.10
  158.2 55.4 all-gather.12
  215.1 53.7 all-gather.14
  357.3 19.2 reduce-scatter.31
  378.9 18.3 reduce-scatter.29
  400.2 29.5 reduce-scatter.33
  432.1 29.9 reduce-scatter.27
  464.3 50.8 reduce-scatter.43
  517.5 51.7 reduce-scatter.39
  571.5 51.8 reduce-scatter.35
  627.0 32.9 reduce-scatter.49
  663.7 33.3 reduce-scatter.47
  700.0 33.7 reduce-scatter.51
  736.7 34.0 reduce-scatter.45
  774.1 34.5 reduce-scatter.53
  812.0 34.5 reduce-scatter.41
  850.0 34.5 reduce-scatter.37
where the time goes:
time: 902 us; the launch traced here: 893 us
  waiting for transfers between devices  451 us (50%)
  blocking collectives  165 us (18%)
  matrix products  131 us (15%)
  other arithmetic  56.3 us (6%)
  local copies, waits for them, and re-layouts  48 us (5%)
  starting transfers between devices  23.1 us (3%)
  between operations  18.3 us (2%)
    unnamed x25, waiting for transfers between devices  161 us
    reduce_scatter x1, waiting for transfers between devices, local(): lax.psum_scatter(sum_up.astype(jnp.bfloat16), 'seq', scatter_dimension=0,...  47.9 us
    reduce_scatter x1, waiting for transfers between devices, local(): lax.psum_scatter(sum_down.astype(jnp.bfloat16), 'seq', scatter_dimension=...  47.7 us
    reduce_scatter x1, waiting for transfers between devices, local(): lax.psum_scatter(sum_gate.astype(jnp.bfloat16), 'seq', scatter_dimension=...  39.6 us
    reduce_scatter x1, waiting for transfers between devices, local(): lax.psum_scatter(rows_gate.astype(jnp.bfloat16), 'dp', scatter_dimension=...  36.4 us
    dot_general x14, matrix products, product(): result = jnp.dot(flat_left, right_side, preferred_element_type=jnp.float32)  36.3 us
    reduce_scatter x1, waiting for transfers between devices, local(): lax.psum_scatter(rows_up.astype(jnp.bfloat16), 'dp', scatter_dimension=1,...  36.1 us
    unnamed x352, local copies, waits for them, and re-layouts  35.5 us
  transfers between devices with their start and end apart: 28, of which 15 were waited for; matrix products, arithmetic and copies ran while one was open for 20% of the time, Pallas kernels for 0%

commit v1 on v0

v1 whole, which is shorter than its diff:
```python
import jax
import jax.numpy as jnp
from jax import lax
from jax.sharding import PartitionSpec as P

D = 640
HEADS = 4
HD = 256
WINDOW = 512
MB = 2


EPS = 1e-06
MASKED = -1e30


def shifted(value, axis, steps):
    count = lax.axis_size(axis)
    first, last = (max(0, -steps), min(count, count - steps))
    return lax.ppermute(value, axis, [(source, source + steps) for source in range(first, last)])


def rms_norm(vector, scale_gain):
    factor = lax.rsqrt(jnp.mean(vector * vector, axis=-1, keepdims=True) + EPS)
    return vector * factor * (1.0 + scale_gain)


def angles(positions, head_width):
    ladder = jnp.arange(head_width // 2).astype(jnp.float32) * 2.0
    inverse = 10000.0 ** (-ladder / head_width)
    return positions[:, None] * inverse[None, :]


def rotate(vector, angle_table):
    middle_at = vector.shape[-1] // 2
    leading = vector[..., :middle_at]
    trailing = vector[..., middle_at:]
    cosine = jnp.cos(angle_table)
    sine_of = jnp.sin(angle_table)
    return jnp.concatenate(
        [leading * cosine - trailing * sine_of, trailing * cosine + leading * sine_of], axis=-1
    )


def gated_unit(gate_val, up_val):
    return jax.nn.gelu(gate_val, approximate=True) * up_val


def product(left_side, right_side):
    flat_left = left_side.reshape(-1, left_side.shape[-1])
    result = jnp.dot(flat_left, right_side, preferred_element_type=jnp.float32)
    return result.reshape(left_side.shape[:-1] + (right_side.shape[-1],))


def outer_sum(left_side, right_side):
    flat_left = left_side.reshape(-1, left_side.shape[-1])
    flat_right = right_side.reshape(-1, right_side.shape[-1])
    return lax.dot_general(
        flat_left, flat_right, (((0,), (0,)), ((), ())), preferred_element_type=jnp.float32
    )


def back_product(gradient, weight):
    flat_grad = gradient.reshape(-1, gradient.shape[-1])
    result = lax.dot_general(
        flat_grad, weight, (((1,), (1,)), ((), ())), preferred_element_type=jnp.float32
    )
    return result.reshape(gradient.shape[:-1] + (weight.shape[0],))


def local_grads(function, primals, cotangent_in):
    return jax.vjp(function, *primals)[1](cotangent_in)


def split_gains(full_gains):
    flat_gains = full_gains.astype(jnp.float32).reshape(-1)
    return (
        flat_gains[0:D],
        flat_gains[D : 2 * D],
        flat_gains[2 * D : 3 * D],
        flat_gains[3 * D : 4 * D],
        flat_gains[4 * D : 4 * D + HD],
        flat_gains[4 * D + HD : 4 * D + 2 * HD],
    )


def masked_scores(queries, key_block, query_pos, key_pos):
    scores = jnp.einsum(
        "sqhd,skd->shqk", queries, key_block, preferred_element_type=jnp.float32
    ) * HD ** (-0.5)
    distance = query_pos[:, None] - key_pos[None, :]
    allowed = (distance >= 0) & (distance < WINDOW) & (key_pos[None, :] >= 0)
    return jnp.where(allowed[None, None], scores, MASKED)


def rms_back(vector, scale_gain, gradient):
    factor = lax.rsqrt(jnp.mean(vector * vector, axis=-1, keepdims=True) + EPS)
    scaled = vector * factor
    inner = gradient * (1.0 + scale_gain)
    d_vector = factor * (inner - scaled * jnp.mean(inner * scaled, axis=-1, keepdims=True))
    d_gain = jnp.sum(gradient * scaled, axis=tuple(range(vector.ndim - 1)))
    return d_vector, d_gain


def columns_joined(gathered):
    seqs, dps, rows, cols = gathered.shape
    return gathered.transpose(0, 2, 1, 3).reshape(seqs * rows, dps * cols)


def rows_joined(gathered):
    seqs, dps, rows, cols = gathered.shape
    return gathered.transpose(1, 2, 0, 3).reshape(dps * rows, seqs * cols)


def columns_parted(whole, seqs, dps):
    rows, cols = whole.shape
    return whole.reshape(seqs, rows // seqs, dps, cols // dps).transpose(2, 0, 1, 3)


def rows_parted(whole, seqs, dps):
    rows, cols = whole.shape
    return whole.reshape(dps, rows // dps, seqs, cols // seqs).transpose(0, 2, 1, 3)


def gather(packed):
    return lax.all_gather(packed, ("seq", "dp")).reshape(
        (lax.axis_size("seq"), lax.axis_size("dp")) + packed.shape
    )


def scatter(packed):
    return lax.psum_scatter(lax.psum_scatter(packed, "dp"), "seq")


def local(inputs, cotangent, w_query, w_key, w_value, w_out, w_gate, w_up, w_down, gains):
    groups, stretch_len = inputs.shape[:2]
    seqs, dps = lax.axis_size("seq"), lax.axis_size("dp")
    heads_width = HEADS * HD
    seq_index = lax.axis_index("seq")
    query_pos = seq_index * stretch_len + jnp.arange(stretch_len, dtype=jnp.int32)
    angle_table = angles(query_pos.astype(jnp.float32), HD)
    reach = WINDOW // stretch_len
    key_pos = (seq_index - reach) * stretch_len + jnp.arange(
        WINDOW + stretch_len, dtype=jnp.int32
    )
    rows_a, cols_q = w_query.shape
    cols_k = w_key.shape[1]
    rows_o = w_out.shape[1]
    rows_g, cols_g = gains.shape
    lead = cols_q + 2 * cols_k
    width = max(-(-(lead + cols_g) // 128) * 128, w_out.shape[0])

    def widened(value, rows, cols):
        return jnp.pad(value, ((0, rows - value.shape[0]), (0, cols - value.shape[1])))

    packed_one = jnp.concatenate(
        [
            widened(
                jnp.concatenate(
                    [w_query, w_key, w_value, widened(gains, rows_a, cols_g)], axis=1
                ),
                rows_a,
                width,
            ),
            widened(w_out.T, rows_o, width),
        ],
        axis=0,
    )
    cols_f = w_gate.shape[1]
    wide = max(2 * cols_f, w_down.shape[0])
    packed_two = jnp.concatenate(
        [
            widened(jnp.concatenate([w_gate, w_up], axis=1), rows_a, wide),
            widened(w_down.T, rows_o, wide),
        ],
        axis=0,
    )
    first = gather(packed_one)
    packed_two, first = lax.optimization_barrier((packed_two, first))
    second = gather(packed_two)

    full_query = columns_joined(first[:, :, :rows_a, :cols_q])
    full_key = columns_joined(first[:, :, :rows_a, cols_q : cols_q + cols_k])
    full_value = columns_joined(first[:, :, :rows_a, cols_q + cols_k : lead])
    full_gains = columns_joined(first[:, :, :rows_g, lead : lead + cols_g])
    out_t = rows_joined(first[:, :, rows_a:, : w_out.shape[0]])
    full_gate = columns_joined(second[:, :, :rows_a, :cols_f])
    full_up = columns_joined(second[:, :, :rows_a, cols_f : 2 * cols_f])
    down_t = rows_joined(second[:, :, rows_a:, : w_down.shape[0]])
    g_attn_in, g_attn_out, g_ffw_in, g_ffw_out, g_query, g_key = split_gains(full_gains)

    resid = inputs.astype(jnp.float32)
    normed = rms_norm(resid, g_attn_in).astype(jnp.bfloat16)
    q_lin = product(normed, full_query).reshape(groups, stretch_len, HEADS, HD)
    k_lin = product(normed, full_key)
    v_lin = product(normed, full_value)
    keys = rotate(rms_norm(k_lin, g_key), angle_table).astype(jnp.bfloat16)
    own = jnp.concatenate([keys, v_lin.astype(jnp.bfloat16)], axis=-1)
    parts = [own]
    for offset in range(1, reach + 1):
        parts.insert(0, shifted(own, "seq", offset))
    queries = rotate(rms_norm(q_lin, g_query), angle_table[:, None, :]).astype(jnp.bfloat16)
    block = jnp.concatenate(parts, axis=1)
    key_block, value_block = block[..., :HD], block[..., HD:]

    scores = masked_scores(queries, key_block, query_pos, key_pos)
    row_max = jnp.max(scores, axis=-1, keepdims=True)
    exponent = jnp.exp(scores - row_max)
    row_sum = jnp.sum(exponent, axis=-1, keepdims=True)
    probs = (exponent / row_sum).astype(jnp.bfloat16)
    log_sum = row_max + jnp.log(row_sum)
    mixed = jnp.einsum(
        "shqk,skd->sqhd", probs, value_block, preferred_element_type=jnp.float32
    )
    mixed = mixed.reshape(groups, stretch_len, heads_width).astype(jnp.bfloat16)

    attended = back_product(mixed, out_t)
    middle = resid + rms_norm(attended, g_attn_out)
    ffw_in = rms_norm(middle, g_ffw_in).astype(jnp.bfloat16)
    gate_val = product(ffw_in, full_gate)
    up_val = product(ffw_in, full_up)
    hidden = gated_unit(gate_val, up_val).astype(jnp.bfloat16)
    down_val = back_product(hidden, down_t)
    outputs = (middle + rms_norm(down_val, g_ffw_out)).astype(jnp.bfloat16)

    grad_out_f = cotangent.astype(jnp.float32)
    d_down, d_g_ffw_out = rms_back(down_val, g_ffw_out, grad_out_f)
    d_down = d_down.astype(jnp.bfloat16)
    d_hidden = product(d_down, down_t)
    d_gate, d_up = local_grads(gated_unit, (gate_val, up_val), d_hidden)
    d_gate = d_gate.astype(jnp.bfloat16)
    d_up = d_up.astype(jnp.bfloat16)
    d_ffw_in = back_product(d_gate, full_gate) + back_product(d_up, full_up)
    d_middle, d_g_ffw_in = rms_back(middle, g_ffw_in, d_ffw_in)
    d_middle = grad_out_f + d_middle
    d_attended, d_g_attn_out = rms_back(attended, g_attn_out, d_middle)
    d_attended = d_attended.astype(jnp.bfloat16)
    d_mixed = (
        product(d_attended, out_t)
        .astype(jnp.bfloat16)
        .reshape(groups, stretch_len, HEADS, HD)
    )
    low = jnp.bfloat16
    sum_gate = columns_parted(outer_sum(ffw_in, d_gate).astype(low), seqs, dps)
    sum_up = columns_parted(outer_sum(ffw_in, d_up).astype(low), seqs, dps)
    sum_down = rows_parted(outer_sum(d_down, hidden).astype(low), seqs, dps)
    def widened_four(value, rows, cols):
        return jnp.pad(
            value, ((0, 0), (0, 0), (0, rows - value.shape[2]), (0, cols - value.shape[3]))
        )

    early = scatter(
        jnp.concatenate(
            [
                widened_four(jnp.concatenate([sum_gate, sum_up], axis=3), rows_a, wide),
                widened_four(sum_down, rows_o, wide),
            ],
            axis=2,
        )
    )

    scores = masked_scores(queries, key_block, query_pos, key_pos)
    full_probs = jnp.exp(scores - log_sum)
    d_probs = jnp.einsum(
        "sqhd,skd->shqk", d_mixed, value_block, preferred_element_type=jnp.float32
    )
    d_scores = full_probs * (d_probs - jnp.sum(full_probs * d_probs, axis=-1, keepdims=True))
    d_scores = d_scores.astype(jnp.bfloat16)
    d_value_block = jnp.einsum(
        "shqk,sqhd->skd",
        full_probs.astype(jnp.bfloat16),
        d_mixed,
        preferred_element_type=jnp.float32,
    )
    d_key_block = jnp.einsum(
        "shqk,sqhd->skd", d_scores, queries, preferred_element_type=jnp.float32
    ) * HD ** (-0.5)
    d_queries = jnp.einsum(
        "shqk,skd->sqhd", d_scores, key_block, preferred_element_type=jnp.float32
    ) * HD ** (-0.5)
    d_block = jnp.concatenate([d_key_block, d_value_block], axis=-1)
    d_own = d_block[:, reach * stretch_len :]
    for offset in range(1, reach + 1):
        at = (reach - offset) * stretch_len
        d_own = d_own + shifted(
            d_block[:, at : at + stretch_len].astype(low), "seq", -offset
        ).astype(jnp.float32)

    def unrotate(gradient, table):
        return rotate(gradient, -table)

    d_q_lin, d_g_query = rms_back(q_lin, g_query, unrotate(d_queries, angle_table[:, None, :]))
    d_k_lin, d_g_key = rms_back(k_lin, g_key, unrotate(d_own[..., :HD], angle_table))
    d_q_lin = d_q_lin.reshape(groups, stretch_len, heads_width).astype(low)
    d_k_lin = d_k_lin.astype(low)
    d_values = d_own[..., HD:].astype(low)
    sum_query = columns_parted(outer_sum(normed, d_q_lin).astype(low), seqs, dps)
    sum_key = columns_parted(outer_sum(normed, d_k_lin).astype(low), seqs, dps)
    sum_value = columns_parted(outer_sum(normed, d_values).astype(low), seqs, dps)
    sum_out = rows_parted(outer_sum(d_attended, mixed).astype(low), seqs, dps)
    d_normed = (
        back_product(d_q_lin, full_query)
        + back_product(d_k_lin, full_key)
        + back_product(d_values, full_value)
    )
    d_resid, d_g_attn_in = rms_back(resid, g_attn_in, d_normed)
    grad_inputs = (d_middle + d_resid).astype(jnp.bfloat16)
    sum_gains = jnp.concatenate(
        [d_g_attn_in, d_g_attn_out, d_g_ffw_in, d_g_ffw_out, d_g_query, d_g_key]
    ).reshape(full_gains.shape)
    sum_gains = columns_parted(sum_gains.astype(low), seqs, dps)

    late = scatter(
        jnp.concatenate(
            [
                widened_four(
                    jnp.concatenate(
                        [sum_query, sum_key, sum_value, widened_four(sum_gains, rows_a, cols_g)],
                        axis=3,
                    ),
                    rows_a,
                    width,
                ),
                widened_four(sum_out, rows_o, width),
            ],
            axis=2,
        )
    )
    early = early.astype(jnp.float32)
    late = late.astype(jnp.float32)
    return (
        outputs,
        grad_inputs,
        late[:rows_a, :cols_q],
        late[:rows_a, cols_q : cols_q + cols_k],
        late[:rows_a, cols_q + cols_k : lead],
        late[rows_a:, : w_out.shape[0]].T,
        early[:rows_a, :cols_f],
        early[:rows_a, cols_f : 2 * cols_f],
        early[rows_a:, : w_down.shape[0]].T,
        late[:rows_g, lead : lead + cols_g],
    )


def solution(mesh):
    in_specs = (
        P("dp", "seq", None),
        P("dp", "seq", None),
        P("seq", "dp"),
        P("seq", "dp"),
        P("seq", "dp"),
        P("seq", "dp"),
        P("seq", "dp"),
        P("seq", "dp"),
        P("seq", "dp"),
        P("seq", "dp"),
    )
    out_specs = (
        P("dp", "seq", None),
        P("dp", "seq", None),
        P("seq", "dp"),
        P("seq", "dp"),
        P("seq", "dp"),
        P("seq", "dp"),
        P("seq", "dp"),
        P("seq", "dp"),
        P("seq", "dp"),
        P("seq", "dp"),
    )
    return jax.shard_map(local, mesh=mesh, in_specs=in_specs, out_specs=out_specs, check_vma=False)
```

time: 902 us -> 563 us (0.62)
  waiting for transfers between devices: 451 us -> 226 us
  blocking collectives: 165 us -> 0 us
  local copies, waits for them, and re-layouts: 48 us -> 115 us
  starting transfers between devices: 23.1 us -> 6.12 us
    unnamed x25 -> x6, waiting for transfers between devices: 161 us -> 0.1 us
    all_gather x11 -> x0, blocking collectives: 139 us -> none  [the longest x1 23 us: collect(): lax.all_gather(part_value, 'seq', axis=0, tiled=True)]
    reduce_scatter x9 -> x4, waiting for transfers between devices: 246 us -> 146 us  [scatter(): return lax.psum_scatter(lax.psum_scatter(packed, 'dp'), 'seq')]
    reshape x0 -> x19, local copies, waits for them, and re-layouts: none -> 45.9 us  [the longest x7 16.7 us: columns_joined(): return gathered.transpose(0, 2, 1, 3).reshape(seqs * rows, dps * cols)]
    all_gather x5 -> x2, waiting for transfers between devices: 31.2 us -> 62.3 us  [gather(): lax.all_gather(packed, ('seq', 'dp'))]
    unnamed x2 -> x0, blocking collectives: 25.8 us -> none
    optimization_barrier x0 -> x3, local copies, waits for them, and re-layouts: none -> 18.1 us  [local(): packed_two, first = lax.optimization_barrier((packed_two, first))]
    convert_element_type x7 -> x10, other arithmetic: 9.38 us -> 23.8 us  [the longest x1 11.7 us: local(): d_scores = d_scores.astype(jnp.bfloat16)]
  transfers between devices with their start and end apart: 28 -> 8, of which waited for: 15 -> 7; matrix products, arithmetic and copies ran while one was open for 20% -> 27% of each run, Pallas kernels for 0% -> 0%
where the time goes in v1:
time: 563 us; the launch traced here: 553 us
  waiting for transfers between devices  226 us (40%)
  matrix products  125 us (22%)
  local copies, waits for them, and re-layouts  115 us (20%)
  other arithmetic  65.2 us (12%)
  between operations  15.5 us (3%)
  starting transfers between devices  6.12 us (1%)
    reduce_scatter x4, waiting for transfers between devices, scatter(): return lax.psum_scatter(lax.psum_scatter(packed, 'dp'), 'seq')  146 us
    all_gather x2, waiting for transfers between devices, gather(): lax.all_gather(packed, ('seq', 'dp'))  62.3 us
    dot_general x7, matrix products, product(): result = jnp.dot(flat_left, right_side, preferred_element_type=jnp.float32)  32.4 us
    unnamed x158, local copies, waits for them, and re-layouts  25.5 us
    dot_general x7, matrix products, outer_sum(): lax.dot_general(flat_left, flat_right, (((0,), (0,)), ((), ())), preferre...  24 us
    dot_general x7, matrix products, back_product(): lax.dot_general(flat_grad, weight, (((1,), (1,)), ((), ())), preferred_el...  20.3 us
    ppermute x2, waiting for transfers between devices, shifted(): lax.ppermute(value, axis, [(source, source + steps) for source in range(f...  18.1 us
    optimization_barrier x3, local copies, waits for them, and re-layouts, local(): packed_two, first = lax.optimization_barrier((packed_two, first))  18.1 us
  transfers between devices with their start and end apart: 8, of which 7 were waited for; matrix products, arithmetic and copies ran while one was open for 27% of the time, Pallas kernels for 0%

profile of v1, /device:TPU:0, one launch (start us, length us, event | category | flops | bytes accessed | tf_op | source)
XLA Modules:
  0.0 553.1 jit_solution(1241338017962904499)
XLA Ops:
  13.7 62.3 %all-gather.5.cloned.1.call-done = bf16[7680,256]{1,0:T(8,128)(2,1)} async-done(((bf16[240,256]{1,0:T(8,128)(2,1)}), bf16[7680,256]{1,0:T(8,128)(2,1)}) %all-gather.5.cloned.1.call-update) | async-done | bytes 3932176 | tf_op jit(solution)/shard_map/all_gather | solution.py:126
  82.2 7.4 %copy.175 = bf16[4,8,240,256]{2,0,3,1:T(4,128)(2,1)} copy(bf16[4,8,240,256]{3,2,1,0:T(8,128)(2,1)} %bitcast.210) | data formatting | bytes 7864320 | tf_op jit(solution)/shard_map/optimization_barrier | solution.py:179
  89.6 5.7 %copy.180 = bf16[4,8,240,256]{3,1,2,0:T(8,128)(2,1)} copy(bf16[4,8,240,256]{3,2,1,0:T(8,128)(2,1)} %bitcast.211) | data formatting | bytes 7864320 | tf_op jit(solution)/shard_map/optimization_barrier | solution.py:179
  95.3 5.0 copy.186
  108.7 4.6 collective-permute-start
  135.3 16.9 %collective-permute-done = bf16[2,512,512]{1,2,0:T(8,128)(2,1)} collective-permute-done((bf16[2,512,512]{1,2,0:T(8,128)(2,1)}, bf16[2,512,512]{1,2,0:T(8,128)(2,1)}, u32[]{:S(2)}, u32[]{:S(2)}) %collective-permute-start) | collective-permute-done | bytes 1048608 | tf_op jit(solution)/shard_map/ppermute | solution.py:20
  153.8 7.7 %fusion.78 = (f32[2,4,512]{2,1,0:T(4,128)S(1)}, f32[2,4,512,1024]{2,3,1,0:T(8,128)}) fusion(bf16[2,512,4,128]{1,3,2,0:T(8,128)(2,1)S(1)} %get-tuple-element.76, bf16[2,512,4,128]{1,3,2,0:T(8,128)(2,1)S(1)} %get-tuple-element.75, bf16[2,1024,512]{1,2,0:T(8,128)(2,1)S(1)} %maximum_maximum_fusion, pred[512,1024]{0,1:T(8,128)(4,1)S(1)} %copy-done.47), kind=kOutput, calls=%fused_computation.188 | convolution fusion | flops 2164256768 | bytes 20463616 | tf_op jit(solution)/shard_map/sqhd,skd->shqk/dot_general | solution.py:88
  161.5 8.1 %fusion.3 = f32[2,4,512]{2,1,0:T(4,128)S(1)} fusion(f32[2,4,512,1024]{2,3,1,0:T(8,128)} %get-tuple-element.110, f32[2,4,512]{2,1,0:T(4,128)S(1)} %get-tuple-element.109), kind=kLoop, calls=%fused_computation.9 | loop fusion | flops 8384512 | bytes 16809984 | tf_op jit(solution)/shard_map/reduce_sum | solution.py:209
  169.6 8.9 %fusion.43 = bf16[2,256,4,512]{3,1,2,0:T(8,128)(2,1)S(1)} fusion(f32[2,4,512,1024]{2,3,1,0:T(8,128)} %get-tuple-element.110, f32[2,4,512]{2,1,0:T(4,128)S(1)} %fusion.3, f32[2,4,512]{2,1,0:T(4,128)S(1)} %get-tuple-element.109, bf16[2,1024,512]{1,2,0:T(8,128)(2,1)S(1)} %maximum_maximum_fusion), kind=kOutput, calls=%fused_computation.103 | convolution fusion | flops 2161115136 | bytes 19955712 | tf_op jit(solution)/shard_map/shqk,skd->sqhd/dot_general | solution.py:212
  189.8 6.0 %copy_bitcast_fusion.1 = (bf16[4,160,8,256]{3,2,1,0:T(8,128)(2,1)}, bf16[4,160,8,256]{3,2,1,0:T(8,128)(2,1)}) fusion(bf16[4,8,160,256]{3,2,1,0:T(8,128)(2,1)S(1)} %get-tuple-element.72, bf16[4,8,160,256]{3,2,1,0:T(8,128)(2,1)S(1)} %get-tuple-element.71), kind=kLoop, calls=%fused_computation.72 | loop fusion | bytes 10485760 | tf_op jit(solution)/shard_map/transpose | solution.py:107
  195.8 5.3 reshape.614
  201.1 5.3 reshape.615
  206.4 5.2 copy.288
  211.7 5.5 reshape.616
  217.1 5.7 %fusion.79 = f32[2,512,2048]{2,1,0:T(8,128)S(1)} fusion(bf16[2,512,640]{2,1,0:T(8,128)(2,1)} %multiply_convert_fusion.4, bf16[640,2048,1]{1,0,2:T(8,128)(2,1)} %reshape.614), kind=kOutput, calls=%fused_computation.189 | convolution fusion | flops 2684354560 | bytes 12320768 | tf_op jit(solution)/shard_map/dot_general | solution.py:51
  222.9 7.1 %multiply_convert_fusion.1 = (bf16[2,512,2048]{2,1,0:T(8,128)(2,1)S(1)}, f32[2,512,2048]{2,1,0:T(8,128)}) fusion(f32[2,512,2048]{2,1,0:T(8,128)S(1)} %fusion.79, bf16[2,512,640]{2,1,0:T(8,128)(2,1)S(1)} %copy-done.41, bf16[640,2048,1]{1,0,2:T(8,128)(2,1)S(1)} %copy-done.19), kind=kOutput, calls=%fused_computation.24 | convolution fusion | flops 2705326080 | bytes 24903680 | tf_op jit(solution)/shard_map/dot_general | solution.py:51
  236.6 12.6 %multiply_convert_fusion = (bf16[2,512,2048]{2,1,0:T(8,128)(2,1)S(1)}, bf16[2,512,2048]{2,1,0:T(8,128)(2,1)S(1)}) fusion(f32[2,512,2048]{2,1,0:T(8,128)} %copy-done.67, f32[2,512,2048]{2,1,0:T(8,128)} %get-tuple-element.114, bf16[2,512,640]{2,1,0:T(8,128)(2,1)S(1)} %get-tuple-element.81, bf16[640,2048,1]{1,0,2:T(8,128)(2,1)S(1)} %copy-done.21), kind=kOutput, calls=%fused_computation.23 | convolution fusion | flops 2734686208 | bytes 29097984 | tf_op jit(solution)/shard_map/dot_general | solution.py:51
  265.3 7.9 %fusion.44 = f32[2,1024,256]{1,2,0:T(8,128)S(1)} fusion(bf16[2,512,4,256]{1,3,2,0:T(8,128)(2,1)} %bitcast.221, f32[2,4,512,1024]{2,3,1,0:T(8,128)} %get-tuple-element.110, f32[2,4,512]{2,1,0:T(4,128)S(1)} %bitcast.238), kind=kOutput, calls=%fused_computation.105 | convolution fusion | flops 2155872256 | bytes 20987904 | tf_op jit(solution)/shard_map/shqk,sqhd->skd/dot_general | solution.py:269
  273.2 15.6 %fusion = (f32[2,4,512]{2,1,0:T(4,128)S(1)}, f32[2,1024,512,4]{2,1,3,0:T(8,128)}) fusion(f32[2,4,512,1024]{2,3,1,0:T(8,128)} %get-tuple-element.110, f32[2,4,512]{2,1,0:T(4,128)S(1)} %bitcast.239, bf16[2,512,4,256]{1,3,2,0:T(8,128)(2,1)} %bitcast.222, bf16[2,1024,512]{1,2,0:T(8,128)(2,1)} %copy-done.18), kind=kOutput, calls=%fused_computation.2 | convolution fusion | flops 2160062464 | bytes 36732928 | tf_op jit(solution)/shard_map/sqhd,skd->shqk/dot_general | solution.py:264
  288.8 11.7 %fusion.2 = bf16[2,4,512,1024]{2,3,1,0:T(8,128)(2,1)S(1)} fusion(f32[2,1024,512,4]{2,1,3,0:T(8,128)} %get-tuple-element.119, f32[2,4,512,1024]{2,3,1,0:T(8,128)} %get-tuple-element.110, f32[2,4,512]{2,1,0:T(4,128)S(1)} %get-tuple-element.118, f32[2,4,512]{2,1,0:T(4,128)S(1)} %bitcast.240), kind=kLoop, calls=%fused_computation.4 | loop fusion | flops 16777216 | bytes 41975808 | tf_op jit(solution)/shard_map/convert_element_type | solution.py:268
  304.4 4.3 multiply_bitcast_fusion
  319.3 4.6 copy.207
  323.9 4.6 bitcast_convert_fusion.3
  332.3 4.1 copy.219
  336.4 3.9 fusion.81
  360.3 6.6 %bitcast_convert_fusion = bf16[640,2048]{1,0:T(8,128)(2,1)} fusion(bf16[2,512,640]{2,1,0:T(8,128)(2,1)S(1)} %copy-done.37, bf16[2,512,2048]{2,1,0:T(8,128)(2,1)} %copy-done.63), kind=kOutput, calls=%fused_computation.31 | convolution fusion | flops 2685665280 | bytes 8126464 | tf_op jit(solution)/shard_map/dot_general | solution.py:58
  366.9 4.3 reshape.601
  372.6 5.5 bitcast_convert_fusion.1
  389.9 30.2 %reduce-scatter.5.cloned.1.call-done = bf16[1,4,240,256]{2,3,1,0:T(8,128)(2,1)} async-done(((bf16[8,4,240,256]{2,3,1,0:T(8,128)(2,1)}), bf16[1,4,240,256]{2,3,1,0:T(8,128)(2,1)}) %reduce-scatter.5.cloned.1.call-update) | async-done | bytes 491536 | tf_op jit(solution)/shard_map/reduce_scatter | solution.py:132
  420.1 73.0 %reduce-scatter.9.cloned.1.call-done = bf16[1,4,240,512]{3,2,1,0:T(8,128)(2,1)} async-done(((bf16[8,4,240,512]{3,2,1,0:T(8,128)(2,1)}), bf16[1,4,240,512]{3,2,1,0:T(8,128)(2,1)}) %reduce-scatter.9.cloned.1.call-update) | async-done | bytes 983056 | tf_op jit(solution)/shard_map/reduce_scatter | solution.py:132
  497.1 19.9 %reduce-scatter.7.cloned.1.call-done = bf16[1,240,256]{1,2,0:T(8,128)(2,1)} async-done(((bf16[4,240,256]{1,2,0:T(8,128)(2,1)}), bf16[1,240,256]{1,2,0:T(8,128)(2,1)}) %reduce-scatter.7.cloned.1.call-update) | async-done | bytes 122896 | tf_op jit(solution)/shard_map/reduce_scatter | solution.py:132
  520.7 22.9 %reduce-scatter.11.cloned.1.call-done = bf16[1,240,512]{2,1,0:T(8,128)(2,1)} async-done(((bf16[4,240,512]{2,1,0:T(8,128)(2,1)}), bf16[1,240,512]{2,1,0:T(8,128)(2,1)}) %reduce-scatter.11.cloned.1.call-update) | async-done | bytes 245776 | tf_op jit(solution)/shard_map/reduce_scatter | solution.py:132
  (283 shorter events, 139.4 us)
Async XLA Ops:
  7.2 68.9 %all-gather.5.cloned.1.call-start = ((), (), s32[]{:S(2)}) async-start(), calls=%async_computation.8 | async-start | bytes 4055040 | tf_op jit(solution)/shard_map/all_gather | solution.py:126
  12.0 171.4 %all-gather.7.cloned.1.call-start = ((), (), s32[]{:S(2)}) async-start(), calls=%async_computation.9 | async-start | bytes 8110080 | tf_op jit(solution)/shard_map/all_gather | solution.py:126
  76.1 344.0 %reduce-scatter.5.cloned.1.call-start = ((), (), s32[]{:S(2)}) async-start(), calls=%async_computation.4 | async-start | bytes 4718592 | tf_op jit(solution)/shard_map/reduce_scatter | solution.py:132
  77.8 42.2 %copy-start.55 = (f32[2,512]{1,0:T(2,128)}, f32[2,512]{1,0:T(2,128)S(1)}, u32[]{:S(2)}) copy-start(f32[2,512]{1,0:T(2,128)S(1)} %add_rsqrt_fusion.5) | copy-start | bytes 12292
  89.6 5.7 %copy-start.1 = (bf16[7680,256]{1,0:T(8,128)(2,1)S(1)}, bf16[7680,256]{1,0:T(8,128)(2,1)}, u32[]{:S(2)}) copy-start(bf16[7680,256]{1,0:T(8,128)(2,1)} %all-gather.5.cloned.1.call-done) | copy-start | bytes 11796484
  100.2 4.6 copy-start.6
  101.6 18.4 %copy-start.53 = (f32[640]{0:T(1024)}, f32[640]{0:T(1024)S(1)}, u32[]{:S(2)}) copy-start(f32[640]{0:T(1024)S(1)} %add.218) | copy-start | bytes 7684
  107.5 8.5 %copy-start.33 = (bf16[2,512,256]{1,2,0:T(8,128)(2,1)}, bf16[2,512,256]{1,2,0:T(8,128)(2,1)S(1)}, u32[]{:S(2)}) copy-start(bf16[2,512,256]{1,2,0:T(8,128)(2,1)S(1)} %convolution_convert_fusion.1) | copy-start | bytes 1572868
  108.7 43.5 %collective-permute-start = (bf16[2,512,512]{1,2,0:T(8,128)(2,1)}, bf16[2,512,512]{1,2,0:T(8,128)(2,1)}, u32[]{:S(2)}, u32[]{:S(2)}) collective-permute-start(bf16[2,512,512]{1,2,0:T(8,128)(2,1)} %pad_maximum_fusion.6), channel_id=1, source_target_pairs={{0,1},{1,2},{2,3},{4,5},{5,6},{6,7},{8,9},{9,10},{10,11},{12,13},{... | collective-permute-start | bytes 3145736 | tf_op jit(solution)/shard_map/ppermute | solution.py:20
  124.0 5.5 copy-start.16
  134.6 17.6 %copy-start.27 = (bf16[2,512,128]{1,2,0:T(8,128)(2,1)S(1)}, bf16[2,512,128]{1,2,0:T(8,128)(2,1)}, u32[]{:S(2)}) copy-start(bf16[2,512,128]{1,2,0:T(8,128)(2,1)} %copy-done.26) | copy-start | bytes 786436
  134.6 17.6 %copy-start.34 = (bf16[2,512,256]{1,2,0:T(8,128)(2,1)S(1)}, bf16[2,512,256]{1,2,0:T(8,128)(2,1)}, u32[]{:S(2)}) copy-start(bf16[2,512,256]{1,2,0:T(8,128)(2,1)} %copy-done.33) | copy-start | bytes 1572868
  135.3 26.2 %copy-start.45 = (bf16[2,512,4,128]{1,3,2,0:T(8,128)(2,1)}, bf16[2,512,4,128]{1,3,2,0:T(8,128)(2,1)S(1)}, u32[]{:S(2)}) copy-start(bf16[2,512,4,128]{1,3,2,0:T(8,128)(2,1)S(1)} %get-tuple-element.75) | copy-start | bytes 3145732
  135.3 26.2 %copy-start.46 = (bf16[2,512,4,128]{1,3,2,0:T(8,128)(2,1)}, bf16[2,512,4,128]{1,3,2,0:T(8,128)(2,1)S(1)}, u32[]{:S(2)}) copy-start(bf16[2,512,4,128]{1,3,2,0:T(8,128)(2,1)S(1)} %get-tuple-element.76) | copy-start | bytes 3145732
  135.3 18.5 %copy-start.47 = (pred[512,1024]{0,1:T(8,128)(4,1)S(1)}, pred[512,1024]{0,1:T(8,128)(4,1)}, u32[]{:S(2)}) copy-start(pred[512,1024]{0,1:T(8,128)(4,1)} %fusion.42) | copy-start | bytes 1572868
  153.8 15.8 %copy-start.18 = (bf16[2,1024,512]{1,2,0:T(8,128)(2,1)}, bf16[2,1024,512]{1,2,0:T(8,128)(2,1)S(1)}, u32[]{:S(2)}) copy-start(bf16[2,1024,512]{1,2,0:T(8,128)(2,1)S(1)} %maximum_maximum_fusion) | copy-start | bytes 6291460
  169.6 8.9 %copy-start.38 = (bf16[640,1024,1]{1,0,2:T(8,128)(2,1)S(1)}, bf16[640,1024,1]{1,0,2:T(8,128)(2,1)}, u32[]{:S(2)}) copy-start(bf16[640,1024,1]{1,0,2:T(8,128)(2,1)} %reshape.613) | copy-start | bytes 3932164
  217.1 5.7 %copy-start.19 = (bf16[640,2048,1]{1,0,2:T(8,128)(2,1)S(1)}, bf16[640,2048,1]{1,0,2:T(8,128)(2,1)}, u32[]{:S(2)}) copy-start(bf16[640,2048,1]{1,0,2:T(8,128)(2,1)} %reshape.615) | copy-start | bytes 7864324
  217.1 5.7 %copy-start.41 = (bf16[2,512,640]{2,1,0:T(8,128)(2,1)S(1)}, bf16[2,512,640]{2,1,0:T(8,128)(2,1)}, u32[]{:S(2)}) copy-start(bf16[2,512,640]{2,1,0:T(8,128)(2,1)} %multiply_convert_fusion.4) | copy-start | bytes 3932164
  222.8 7.1 %copy-start.67 = (f32[2,512,2048]{2,1,0:T(8,128)}, f32[2,512,2048]{2,1,0:T(8,128)S(1)}, u32[]{:S(2)}) copy-start(f32[2,512,2048]{2,1,0:T(8,128)S(1)} %fusion.79) | copy-start | bytes 25165828
  222.9 7.1 %copy-start.21 = (bf16[640,2048,1]{1,0,2:T(8,128)(2,1)S(1)}, bf16[640,2048,1]{1,0,2:T(8,128)(2,1)}, u32[]{:S(2)}) copy-start(bf16[640,2048,1]{1,0,2:T(8,128)(2,1)} %reshape.616) | copy-start | bytes 7864324
  229.9 3.7 copy-start.9
  236.6 12.6 %copy-start.36 = (bf16[2,512,640]{2,1,0:T(8,128)(2,1)}, bf16[2,512,640]{2,1,0:T(8,128)(2,1)S(1)}, u32[]{:S(2)}) copy-start(bf16[2,512,640]{2,1,0:T(8,128)(2,1)S(1)} %get-tuple-element.81) | copy-start | bytes 3932164
  236.6 12.6 %copy-start.20 = (bf16[640,2048,1]{1,0,2:T(8,128)(2,1)S(1)}, bf16[640,2048,1]{1,0,2:T(8,128)(2,1)}, u32[]{:S(2)}) copy-start(bf16[640,2048,1]{1,0,2:T(8,128)(2,1)} %reshape.614) | copy-start | bytes 7864324
  252.6 3.9 copy-start.5
  304.4 4.3 copy-start.12
  309.9 31.6 %collective-permute-start.1 = (bf16[2,512,512]{1,2,0:T(8,128)(2,1)}, bf16[2,512,512]{1,2,0:T(8,128)(2,1)}, u32[]{:S(2)}, u32[]{:S(2)}) collective-permute-start(bf16[2,512,512]{1,2,0:T(8,128)(2,1)} %fusion.40), channel_id=1, source_target_pairs={{1,0},{2,1},{3,2},{5,4},{6,5},{7,6},{9,8},{10,9},{11,10},{13,12},{... | collective-permute-start | bytes 3145736 | tf_op jit(solution)/shard_map/ppermute | solution.py:20
  336.4 5.2 copy-start.13
  359.0 134.1 %reduce-scatter.9.cloned.1.call-start = ((), (), s32[]{:S(2)}) async-start(), calls=%async_computation.6 | async-start | bytes 8847360 | tf_op jit(solution)/shard_map/reduce_scatter | solution.py:132
  389.8 103.4 %copy-start.3 = (f32[2,512,640]{2,1,0:T(8,128)S(1)}, f32[2,512,640]{2,1,0:T(8,128)}, u32[]{:S(2)}) copy-start(f32[2,512,640]{2,1,0:T(8,128)} %copy-done.2) | copy-start | bytes 7864324
  389.8 127.1 %reduce-scatter.7.cloned.1.call-start = ((), (), s32[]{:S(2)}) async-start(), calls=%async_computation.5 | async-start | bytes 655360 | tf_op jit(solution)/shard_map/reduce_scatter | solution.py:132
  420.1 123.5 %reduce-scatter.11.cloned.1.call-start = ((), (), s32[]{:S(2)}) async-start(), calls=%async_computation.7 | async-start | bytes 1228800 | tf_op jit(solution)/shard_map/reduce_scatter | solution.py:132
  (44 other events, 88.8 us)
Sparse Core Ops, SparseCore 0:
  12.1 63.8 all-gather.4
  78.9 81.1 all-gather.6
  359.1 60.8 reduce-scatter.4
  423.7 69.3 reduce-scatter.8
  495.3 21.6 reduce-scatter.6
  519.1 24.4 reduce-scatter.10

commit v2 on v1

--- a/solution.py
+++ b/solution.py
@@ -1,6 +1,11 @@
+import functools
+import math
+
 import jax
 import jax.numpy as jnp
 from jax import lax
+from jax.experimental import pallas as pl
+from jax.experimental.pallas import tpu as pltpu
 from jax.sharding import PartitionSpec as P
 
 D = 640
@@ -42,10 +47,6 @@
     )
 
 
-def gated_unit(gate_val, up_val):
-    return jax.nn.gelu(gate_val, approximate=True) * up_val
-
-
 def product(left_side, right_side):
     flat_left = left_side.reshape(-1, left_side.shape[-1])
     result = jnp.dot(flat_left, right_side, preferred_element_type=jnp.float32)
@@ -66,10 +67,6 @@
         flat_grad, weight, (((1,), (1,)), ((), ())), preferred_element_type=jnp.float32
     )
     return result.reshape(gradient.shape[:-1] + (weight.shape[0],))
-
-
-def local_grads(function, primals, cotangent_in):
-    return jax.vjp(function, *primals)[1](cotangent_in)
 
 
 def split_gains(full_gains):
@@ -84,13 +81,262 @@
     )
 
 
-def masked_scores(queries, key_block, query_pos, key_pos):
-    scores = jnp.einsum(
-        "sqhd,skd->shqk", queries, key_block, preferred_element_type=jnp.float32
-    ) * HD ** (-0.5)
-    distance = query_pos[:, None] - key_pos[None, :]
-    allowed = (distance >= 0) & (distance < WINDOW) & (key_pos[None, :] >= 0)
-    return jnp.where(allowed[None, None], scores, MASKED)
+NN = (((1,), (0,)), ((), ()))
+NT = (((1,), (1,)), ((), ()))
+TN = (((0,), (0,)), ((), ()))
+VMEM_BYTES = 60 * 2**20
+
+
+def dot(left_side, right_side, dims):
+    return lax.dot_general(left_side, right_side, dims, preferred_element_type=jnp.float32)
+
+
+def heads_stacked(ref, rows):
+    return jnp.concatenate([ref[0, rows, h * HD : (h + 1) * HD] for h in range(HEADS)], axis=0)
+
+
+def exponentials(base, queries, keys, first):
+    rows, span = queries.shape[0], keys.shape[0]
+    scores = dot(queries, keys, NT) * HD ** (-0.5)
+    row_at = lax.broadcasted_iota(jnp.int32, (rows, span), 0) % (rows // HEADS)
+    key_at = lax.broadcasted_iota(jnp.int32, (rows, span), 1)
+    distance = row_at + WINDOW - key_at
+    allowed = (distance >= 0) & (distance < WINDOW) & (base + first + key_at >= 0)
+    return jnp.where(allowed, jnp.exp(scores), 0.0)
+
+
+def attend_kernel(step, base_ref, q_ref, kv_ref, mixed_ref):
+    length = q_ref.shape[1]
+    for first in range(0, length, step):
+        rows, span = pl.ds(first, step), pl.ds(first, step + WINDOW)
+        queries = heads_stacked(q_ref, rows)
+        exponent = exponentials(base_ref[0], queries, kv_ref[0, span, :HD], first)
+        row_sum = jnp.sum(exponent, axis=-1, keepdims=True)
+        mixed = dot(exponent.astype(jnp.bfloat16), kv_ref[0, span, HD:], NN) / row_sum
+        for h in range(HEADS):
+            mixed_ref[0, rows, h * HD : (h + 1) * HD] = mixed[
+                h * step : (h + 1) * step
+            ].astype(jnp.bfloat16)
+
+
+def attend(base, queries, block):
+    groups, length, wide = queries.shape
+    span = block.shape[1]
+    step = min(256, length)
+    return pl.pallas_call(
+        functools.partial(attend_kernel, step),
+        grid=(groups,),
+        in_specs=[
+            pl.BlockSpec(memory_space=pltpu.SMEM),
+            pl.BlockSpec((1, length, wide), lambda g: (g, 0, 0)),
+            pl.BlockSpec((1, span, 2 * HD), lambda g: (g, 0, 0)),
+        ],
+        out_specs=pl.BlockSpec((1, length, wide), lambda g: (g, 0, 0)),
+        out_shape=jax.ShapeDtypeStruct(queries.shape, jnp.bfloat16),
+        compiler_params=pltpu.CompilerParams(vmem_limit_bytes=VMEM_BYTES),
+        cost_estimate=pl.CostEstimate(
+            flops=4 * groups * length * wide * span, bytes_accessed=8 * 2**20, transcendentals=0
+        ),
+    )(base, queries, block)
+
+
+def attend_back_kernel(step, base_ref, q_ref, kv_ref, d_mixed_ref, d_q_ref, d_kv_ref):
+    length = q_ref.shape[1]
+    d_kv_ref[...] = jnp.zeros_like(d_kv_ref)
+    for first in range(0, length, step):
+        rows, span = pl.ds(first, step), pl.ds(first, step + WINDOW)
+        queries = heads_stacked(q_ref, rows)
+        d_mixed = heads_stacked(d_mixed_ref, rows)
+        keys, values = kv_ref[0, span, :HD], kv_ref[0, span, HD:]
+        exponent = exponentials(base_ref[0], queries, keys, first)
+        probs = exponent * (1.0 / jnp.sum(exponent, axis=-1, keepdims=True))
+        d_probs = dot(d_mixed, values, NT)
+        inner = jnp.sum(probs * d_probs, axis=-1, keepdims=True)
+        d_scores = (probs * (d_probs - inner)).astype(jnp.bfloat16)
+        d_kv_ref[0, span, HD:] += dot(probs.astype(jnp.bfloat16), d_mixed, TN)
+        d_kv_ref[0, span, :HD] += dot(d_scores, queries, TN) * HD ** (-0.5)
+        d_queries = dot(d_scores, keys, NN) * HD ** (-0.5)
+        for h in range(HEADS):
+            d_q_ref[0, rows, h * HD : (h + 1) * HD] = d_queries[h * step : (h + 1) * step]
+
+
+def attend_back(base, queries, block, d_mixed):
+    groups, length, wide = queries.shape
+    span = block.shape[1]
+    step = min(256, length)
+    whole = pl.BlockSpec((1, length, wide), lambda g: (g, 0, 0))
+    ahead = pl.BlockSpec((1, span, 2 * HD), lambda g: (g, 0, 0))
+    return pl.pallas_call(
+        functools.partial(attend_back_kernel, step),
+        grid=(groups,),
+        in_specs=[pl.BlockSpec(memory_space=pltpu.SMEM), whole, ahead, whole],
+        out_specs=[whole, ahead],
+        out_shape=[
+            jax.ShapeDtypeStruct(queries.shape, jnp.float32),
+            jax.ShapeDtypeStruct(block.shape, jnp.float32),
+        ],
+        compiler_params=pltpu.CompilerParams(vmem_limit_bytes=VMEM_BYTES),
+        cost_estimate=pl.CostEstimate(
+            flops=10 * groups * length * wide * span, bytes_accessed=16 * 2**20, transcendentals=0
+        ),
+    )(base, queries, block, d_mixed)
+
+
+def normed_back(vector, factor, plus_gain, gradient):
+    scaled = vector * factor
+    inner = gradient * plus_gain
+    d_vector = factor * (inner - scaled * jnp.mean(inner * scaled, axis=-1, keepdims=True))
+    return d_vector, jnp.sum(gradient * scaled, axis=0, keepdims=True)
+
+
+def factor_of(vector):
+    return lax.rsqrt(jnp.mean(vector * vector, axis=-1, keepdims=True) + EPS)
+
+
+def middle_kernel(
+    sizes, x_ref, cot_ref, mixed_ref, gains_ref, *refs
+):
+    if sizes is None:
+        out_t, gate, up, down_t = refs[:4]
+        outs = refs[4:]
+    else:
+        first, second = refs[:2]
+        outs = refs[2:12]
+        out_t, gate, up, down_t = refs[12:]
+    (
+        y_ref, d_middle_ref, d_mixed_ref, hidden_ref, d_gate_ref, d_up_ref, ffw_in_ref,
+        d_down_ref, d_attended_ref, d_gains_ref,
+    ) = outs
+    low = jnp.bfloat16
+
+    @pl.when(pl.program_id(0) == 0)
+    def _():
+        d_gains_ref[...] = jnp.zeros_like(d_gains_ref)
+        if sizes is not None:
+            rows_a, rows_o, cols_f, cols_o, cols_d = sizes
+            for s in range(first.shape[0]):
+                for d in range(first.shape[1]):
+                    tall, flat = pl.ds(s * rows_a, rows_a), pl.ds(d * rows_o, rows_o)
+                    wide = pl.ds(d * cols_f, cols_f)
+                    gate[tall, wide] = second[s, d, :rows_a, :cols_f]
+                    up[tall, wide] = second[s, d, :rows_a, cols_f : 2 * cols_f]
+                    down_t[flat, pl.ds(s * cols_d, cols_d)] = second[s, d, rows_a:, :cols_d]
+                    out_t[flat, pl.ds(s * cols_o, cols_o)] = first[s, d, :, :cols_o]
+
+    x, grad = x_ref[...].astype(jnp.float32), cot_ref[...].astype(jnp.float32)
+    plus = [1.0 + gains_ref[r : r + 1, :] for r in range(4)]
+    attended = dot(mixed_ref[...], out_t[...], NT)
+    attended_factor = factor_of(attended)
+    middle = x + attended * attended_factor * plus[1]
+    middle_factor = factor_of(middle)
+    ffw_in = (middle * middle_factor * plus[2]).astype(low)
+    ffw_in_ref[...] = ffw_in
+    a = dot(ffw_in, gate[...], NN)
+    b = dot(ffw_in, up[...], NN)
+    slope = math.sqrt(2.0 / math.pi)
+    square = a * a
+    bend = jnp.tanh(slope * a * (1.0 + 0.044715 * square))
+    half = 0.5 * (1.0 + bend)
+    gelu = a * half
+    hidden = (gelu * b).astype(low)
+    hidden_ref[...] = hidden
+    down = dot(hidden, down_t[...], NT)
+    down_factor = factor_of(down)
+    y_ref[...] = (middle + down * down_factor * plus[3]).astype(low)
+    d_down, d_out_gain = normed_back(down, down_factor, plus[3], grad)
+    d_down = d_down.astype(low)
+    d_down_ref[...] = d_down
+    d_hidden = dot(d_down, down_t[...], NN)
+    d_up = (d_hidden * gelu).astype(low)
+    d_up_ref[...] = d_up
+    gelu_slope = half + 0.5 * a * (1.0 - bend * bend) * (
+        slope * (1.0 + 3.0 * 0.044715 * square)
+    )
+    d_gate = (d_hidden * b * gelu_slope).astype(low)
+    d_gate_ref[...] = d_gate
+    d_ffw_in = dot(d_gate, gate[...], NT) + dot(d_up, up[...], NT)
+    d_middle, d_in_gain = normed_back(middle, middle_factor, plus[2], d_ffw_in)
+    d_middle = grad + d_middle
+    d_middle_ref[...] = d_middle
+    d_attended, d_attn_gain = normed_back(attended, attended_factor, plus[1], d_middle)
+    d_attended = d_attended.astype(low)
+    d_attended_ref[...] = d_attended
+    d_mixed_ref[...] = dot(d_attended, out_t[...], NN).astype(low)
+    d_gains_ref[1:2, :] += d_attn_gain
+    d_gains_ref[2:3, :] += d_in_gain
+    d_gains_ref[3:4, :] += d_out_gain
+
+
+def middle_part(x, cot, mixed, gains_four, weights, sizes, ff):
+    tokens = x.shape[0]
+    step = min(256, tokens)
+    low = jnp.bfloat16
+    wide = mixed.shape[1]
+
+    def rows(cols):
+        return pl.BlockSpec((step, cols), lambda i: (i, 0))
+
+    def fixed(shape):
+        return pl.BlockSpec(
+            shape, lambda i: (0,) * len(shape), pipeline_mode=pl.Buffered(1)
+        )
+
+    outs = [
+        (D, low), (D, jnp.float32), (wide, low), (ff, low), (ff, low), (ff, low), (D, low),
+        (D, low), (D, low),
+    ]
+    scratch = []
+    if sizes is not None:
+        scratch = [pltpu.VMEM((D, cols), low) for cols in (wide, ff, ff, ff)]
+    return pl.pallas_call(
+        functools.partial(middle_kernel, sizes),
+        grid=(tokens // step,),
+        in_specs=[rows(D), rows(D), rows(wide), fixed((8, D))]
+        + [fixed(weight.shape) for weight in weights],
+        out_specs=[rows(cols) for cols, _ in outs] + [pl.BlockSpec((8, D), lambda i: (0, 0))],
+        out_shape=[jax.ShapeDtypeStruct((tokens, cols), kind) for cols, kind in outs]
+        + [jax.ShapeDtypeStruct((8, D), jnp.float32)],
+        scratch_shapes=scratch,
+        compiler_params=pltpu.CompilerParams(vmem_limit_bytes=VMEM_BYTES),
+        cost_estimate=pl.CostEstimate(
+            flops=4 * tokens * D * (3 * ff + wide), bytes_accessed=40 * 2**20, transcendentals=0
+        ),
+    )(x, cot, mixed, gains_four, *weights)
+
+
+def sums_kernel(seqs, rows_a, rows_o, cols_f, ffw_in, d_down, d_gate, d_up, hidden, out):
+    at = pl.program_id(0)
+    low = jnp.bfloat16
+    each = d_gate.shape[1] // cols_f
+    for half, gradient in enumerate((d_gate, d_up)):
+        total = dot(ffw_in[...], gradient[...], TN).astype(low)
+        for e in range(each):
+            for s in range(seqs):
+                out[at * each + e, s, :rows_a, half * cols_f : (half + 1) * cols_f] = total[
+                    s * rows_a : (s + 1) * rows_a, e * cols_f : (e + 1) * cols_f
+                ]
+    total = dot(d_down[...], hidden[...], TN).astype(low)
+    for d in range(out.shape[0]):
+        out[d, at, rows_a:, :] = total[d * rows_o : (d + 1) * rows_o, :]
+
+
+def packed_sums(seqs, dps, sizes, ffw_in, d_down, d_gate, d_up, hidden):
+    rows_a, rows_o, cols_f, _, cols_d = sizes
+    tokens = ffw_in.shape[0]
+    shape = (dps, seqs, rows_a + rows_o, cols_d)
+    whole = pl.BlockSpec((tokens, D), lambda i: (0, 0))
+    part = pl.BlockSpec((tokens, cols_d), lambda i: (0, i))
+    return pl.pallas_call(
+        functools.partial(sums_kernel, seqs, rows_a, rows_o, cols_f),
+        grid=(seqs,),
+        in_specs=[whole, whole, part, part, part],
+        out_specs=pl.BlockSpec(shape, lambda i: (0, 0, 0, 0)),
+        out_shape=jax.ShapeDtypeStruct(shape, jnp.bfloat16),
+        compiler_params=pltpu.CompilerParams(vmem_limit_bytes=VMEM_BYTES),
+        cost_estimate=pl.CostEstimate(
+            flops=6 * tokens * D * cols_d * seqs, bytes_accessed=24 * 2**20, transcendentals=0
+        ),
+    )(ffw_in, d_down, d_gate, d_up, hidden)
 
 
 def rms_back(vector, scale_gain, gradient):
@@ -140,9 +386,6 @@
     query_pos = seq_index * stretch_len + jnp.arange(stretch_len, dtype=jnp.int32)
     angle_table = angles(query_pos.astype(jnp.float32), HD)
     reach = WINDOW // stretch_len
-    key_pos = (seq_index - reach) * stretch_len + jnp.arange(
-        WINDOW + stretch_len, dtype=jnp.int32
-    )
     rows_a, cols_q = w_query.shape
     cols_k = w_key.shape[1]
     rows_o = w_out.shape[1]
@@ -183,10 +426,25 @@
     full_key = columns_joined(first[:, :, :rows_a, cols_q : cols_q + cols_k])
     full_value = columns_joined(first[:, :, :rows_a, cols_q + cols_k : lead])
     full_gains = columns_joined(first[:, :, :rows_g, lead : lead + cols_g])
-    out_t = rows_joined(first[:, :, rows_a:, : w_out.shape[0]])
-    full_gate = columns_joined(second[:, :, :rows_a, :cols_f])
-    full_up = columns_joined(second[:, :, :rows_a, cols_f : 2 * cols_f])
-    down_t = rows_joined(second[:, :, rows_a:, : w_down.shape[0]])
+    cols_o, cols_d = w_out.shape[0], w_down.shape[0]
+    sizes = (rows_a, rows_o, cols_f, cols_o, cols_d)
+    aligned = (
+        rows_a % 16 == 0
+        and rows_o % 16 == 0
+        and cols_f % 128 == 0
+        and cols_o % 128 == 0
+        and cols_d == 2 * cols_f
+        and dps == 2 * seqs
+    )
+    if aligned:
+        weights = (first[:, :, rows_a:, :], second)
+    else:
+        weights = (
+            rows_joined(first[:, :, rows_a:, :cols_o]),
+            columns_joined(second[:, :, :rows_a, :cols_f]),
+            columns_joined(second[:, :, :rows_a, cols_f : 2 * cols_f]),
+            rows_joined(second[:, :, rows_a:, :cols_d]),
+        )
     g_attn_in, g_attn_out, g_ffw_in, g_ffw_out, g_query, g_key = split_gains(full_gains)
 
     resid = inputs.astype(jnp.float32)
@@ -201,84 +459,53 @@
         parts.insert(0, shifted(own, "seq", offset))
     queries = rotate(rms_norm(q_lin, g_query), angle_table[:, None, :]).astype(jnp.bfloat16)
     block = jnp.concatenate(parts, axis=1)
-    key_block, value_block = block[..., :HD], block[..., HD:]
-
-    scores = masked_scores(queries, key_block, query_pos, key_pos)
-    row_max = jnp.max(scores, axis=-1, keepdims=True)
-    exponent = jnp.exp(scores - row_max)
-    row_sum = jnp.sum(exponent, axis=-1, keepdims=True)
-    probs = (exponent / row_sum).astype(jnp.bfloat16)
-    log_sum = row_max + jnp.log(row_sum)
-    mixed = jnp.einsum(
-        "shqk,skd->sqhd", probs, value_block, preferred_element_type=jnp.float32
-    )
-    mixed = mixed.reshape(groups, stretch_len, heads_width).astype(jnp.bfloat16)
-
-    attended = back_product(mixed, out_t)
-    middle = resid + rms_norm(attended, g_attn_out)
-    ffw_in = rms_norm(middle, g_ffw_in).astype(jnp.bfloat16)
-    gate_val = product(ffw_in, full_gate)
-    up_val = product(ffw_in, full_up)
-    hidden = gated_unit(gate_val, up_val).astype(jnp.bfloat16)
-    down_val = back_product(hidden, down_t)
-    outputs = (middle + rms_norm(down_val, g_ffw_out)).astype(jnp.bfloat16)
-
-    grad_out_f = cotangent.astype(jnp.float32)
-    d_down, d_g_ffw_out = rms_back(down_val, g_ffw_out, grad_out_f)
-    d_down = d_down.astype(jnp.bfloat16)
-    d_hidden = product(d_down, down_t)
-    d_gate, d_up = local_grads(gated_unit, (gate_val, up_val), d_hidden)
-    d_gate = d_gate.astype(jnp.bfloat16)
-    d_up = d_up.astype(jnp.bfloat16)
-    d_ffw_in = back_product(d_gate, full_gate) + back_product(d_up, full_up)
-    d_middle, d_g_ffw_in = rms_back(middle, g_ffw_in, d_ffw_in)
-    d_middle = grad_out_f + d_middle
-    d_attended, d_g_attn_out = rms_back(attended, g_attn_out, d_middle)
-    d_attended = d_attended.astype(jnp.bfloat16)
-    d_mixed = (
-        product(d_attended, out_t)
-        .astype(jnp.bfloat16)
-        .reshape(groups, stretch_len, HEADS, HD)
-    )
+
+    base = ((seq_index - reach) * stretch_len).astype(jnp.int32).reshape(1)
     low = jnp.bfloat16
-    sum_gate = columns_parted(outer_sum(ffw_in, d_gate).astype(low), seqs, dps)
-    sum_up = columns_parted(outer_sum(ffw_in, d_up).astype(low), seqs, dps)
-    sum_down = rows_parted(outer_sum(d_down, hidden).astype(low), seqs, dps)
+    tokens = groups * stretch_len
+    queries = queries.reshape(groups, stretch_len, heads_width)
+    mixed = attend(base, queries, block).reshape(tokens, heads_width)
+    gains_four = jnp.pad(
+        jnp.stack([g_attn_in, g_attn_out, g_ffw_in, g_ffw_out]), ((0, 4), (0, 0))
+    )
+    (
+        outputs, d_middle, d_mixed, hidden, d_gate, d_up, ffw_in, d_down, d_attended, d_gains
+    ) = middle_part(
+        inputs.reshape(tokens, D),
+        cotangent.reshape(tokens, D),
+        mixed,
+        gains_four,
+        weights,
+        sizes if aligned else None,
+        cols_f * dps,
+    )
+    outputs = outputs.reshape(inputs.shape)
+    d_middle = d_middle.reshape(inputs.shape)
+    d_mixed = d_mixed.reshape(groups, stretch_len, heads_width)
+
     def widened_four(value, rows, cols):
         return jnp.pad(
             value, ((0, 0), (0, 0), (0, rows - value.shape[2]), (0, cols - value.shape[3]))
         )
 
-    early = scatter(
-        jnp.concatenate(
+    if aligned:
+        early = packed_sums(seqs, dps, sizes, ffw_in, d_down, d_gate, d_up, hidden)
+    else:
+        sum_gate = columns_parted(outer_sum(ffw_in, d_gate).astype(low), seqs, dps)
+        sum_up = columns_parted(outer_sum(ffw_in, d_up).astype(low), seqs, dps)
+        sum_down = rows_parted(outer_sum(d_down, hidden).astype(low), seqs, dps)
+        early = jnp.concatenate(
             [
                 widened_four(jnp.concatenate([sum_gate, sum_up], axis=3), rows_a, wide),
                 widened_four(sum_down, rows_o, wide),
             ],
             axis=2,
         )
-    )
-
-    scores = masked_scores(queries, key_block, query_pos, key_pos)
-    full_probs = jnp.exp(scores - log_sum)
-    d_probs = jnp.einsum(
-        "sqhd,skd->shqk", d_mixed, value_block, preferred_element_type=jnp.float32
-    )
-    d_scores = full_probs * (d_probs - jnp.sum(full_probs * d_probs, axis=-1, keepdims=True))
-    d_scores = d_scores.astype(jnp.bfloat16)
-    d_value_block = jnp.einsum(
-        "shqk,sqhd->skd",
-        full_probs.astype(jnp.bfloat16),
-        d_mixed,
-        preferred_element_type=jnp.float32,
-    )
-    d_key_block = jnp.einsum(
-        "shqk,sqhd->skd", d_scores, queries, preferred_element_type=jnp.float32
-    ) * HD ** (-0.5)
-    d_queries = jnp.einsum(
-        "shqk,skd->sqhd", d_scores, key_block, preferred_element_type=jnp.float32
-    ) * HD ** (-0.5)
-    d_block = jnp.concatenate([d_key_block, d_value_block], axis=-1)
+    early, d_mixed = lax.optimization_barrier((early, d_mixed))
+    early = scatter(early)
+
+    d_queries, d_block = attend_back(base, queries, block, d_mixed)
+    d_queries = d_queries.reshape(groups, stretch_len, HEADS, HD)
     d_own = d_block[:, reach * stretch_len :]
     for offset in range(1, reach + 1):
         at = (reach - offset) * stretch_len
@@ -306,7 +533,7 @@
     d_resid, d_g_attn_in = rms_back(resid, g_attn_in, d_normed)
     grad_inputs = (d_middle + d_resid).astype(jnp.bfloat16)
     sum_gains = jnp.concatenate(
-        [d_g_attn_in, d_g_attn_out, d_g_ffw_in, d_g_ffw_out, d_g_query, d_g_key]
+        [d_g_attn_in, d_gains[1], d_gains[2], d_gains[3], d_g_query, d_g_key]
     ).reshape(full_gains.shape)
     sum_gains = columns_parted(sum_gains.astype(low), seqs, dps)
 

time: 563 us -> 489 us (0.87)
  matrix products: 125 us -> 21.9 us
  Pallas kernels: 0 us -> 80.7 us
  local copies, waits for them, and re-layouts: 115 us -> 67.2 us
  other arithmetic: 65.2 us -> 34.1 us
  waiting for transfers between devices: 226 us -> 257 us
    pallas_call x0 -> x4, Pallas kernels: none -> 80.7 us  [the longest x1 40 us: middle_part(): pl.pallas_call(functools.partial(middle_kernel, sizes), grid=(tokens // s...]
    dot_general x6 -> x0, matrix products: 48.3 us -> none  [the longest x1 15.6 us: local(): jnp.einsum('sqhd,skd->shqk', d_mixed, value_block, preferred_element_type...]
    reduce_scatter x4, waiting for transfers between devices: 146 us -> 176 us  [scatter(): return lax.psum_scatter(lax.psum_scatter(packed, 'dp'), 'seq')]
    dot_general x7 -> x3, matrix products: 32.4 us -> 6.74 us  [product(): result = jnp.dot(flat_left, right_side, preferred_element_type=jnp.float32)]
    optimization_barrier x3 -> x0, local copies, waits for them, and re-layouts: 18.1 us -> none  [local(): packed_two, first = lax.optimization_barrier((packed_two, first))]
    dot_general x7 -> x4, matrix products: 24 us -> 7.98 us  [outer_sum(): lax.dot_general(flat_left, flat_right, (((0,), (0,)), ((), ())), preferre...]
    convert_element_type x4 -> x0, other arithmetic: 15.5 us -> none  [the longest x1 11.7 us: local(): d_scores = d_scores.astype(jnp.bfloat16)]
    unnamed x158 -> x64, local copies, waits for them, and re-layouts: 25.5 us -> 12.3 us
  transfers between devices with their start and end apart: 8 -> 8, of which waited for: 7 -> 7; matrix products, arithmetic and copies ran while one was open for 27% -> 20% of each run, Pallas kernels for 0% -> 2%
where the time goes in v2:
time: 489 us; the launch traced here: 481 us
  waiting for transfers between devices  257 us (53%)
  Pallas kernels  80.7 us (17%)
  local copies, waits for them, and re-layouts  67.2 us (14%)
  other arithmetic  34.1 us (7%)
  matrix products  21.9 us (4%)
  between operations  15 us (3%)
  starting transfers between devices  5.86 us (1%)
    reduce_scatter x4, waiting for transfers between devices, scatter(): return lax.psum_scatter(lax.psum_scatter(packed, 'dp'), 'seq')  176 us
    all_gather x2, waiting for transfers between devices, gather(): lax.all_gather(packed, ('seq', 'dp'))  64.8 us
    pallas_call x1, Pallas kernels, middle_part(): pl.pallas_call(functools.partial(middle_kernel, sizes), grid=(tokens // s...  40 us
    pallas_call x1, Pallas kernels, attend_back(): pl.pallas_call(functools.partial(attend_back_kernel, step), grid=(groups,...  17.4 us
    ppermute x2, waiting for transfers between devices, shifted(): lax.ppermute(value, axis, [(source, source + steps) for source in range(f...  15.2 us
    pallas_call x1, Pallas kernels, packed_sums(): pl.pallas_call(functools.partial(sums_kernel, seqs, rows_a, rows_o, cols_...  15.1 us
    unnamed x64, local copies, waits for them, and re-layouts  12.3 us
  transfers between devices with their start and end apart: 8, of which 7 were waited for; matrix products, arithmetic and copies ran while one was open for 20% of the time, Pallas kernels for 2%

profile of v2, /device:TPU:0, one launch (start us, length us, event | category | flops | bytes accessed | tf_op | source)
XLA Modules:
  0.0 481.4 jit_solution(6043350461802355612)
XLA Ops:
  13.8 62.3 %all-gather.5.cloned.1.call-done = bf16[7680,256]{1,0:T(8,128)(2,1)} async-done(((bf16[240,256]{1,0:T(8,128)(2,1)}), bf16[7680,256]{1,0:T(8,128)(2,1)}) %all-gather.5.cloned.1.call-update) | async-done | bytes 3932176 | tf_op jit(solution)/shard_map/all_gather | solution.py:372
  81.9 2.7 slice.133.refs_0_
  84.5 2.1 slice_bitcast_fusion.1
  103.0 4.3 collective-permute-start
  110.4 3.2 reshape.451
  113.6 2.8 copy.185
  116.4 2.4 copy.129
  118.9 3.3 multiply_reduce_fusion.2
  125.5 2.5 copy.171.q_ref
  129.1 15.2 %collective-permute-done = bf16[2,512,512]{2,1,0:T(8,128)(2,1)} collective-permute-done((bf16[2,512,512]{2,1,0:T(8,128)(2,1)}, bf16[2,512,512]{2,1,0:T(8,128)(2,1)}, u32[]{:S(2)}, u32[]{:S(2)}) %collective-permute-start) | collective-permute-done | bytes 1048608 | tf_op jit(solution)/shard_map/ppermute | solution.py:25
  144.3 3.0 maximum_maximum_fusion.kv_ref
  147.3 8.1 %shard_map.177 = bf16[2,512,1024]{2,1,0:T(8,128)(2,1)} custom-call(s32[1]{0:T(128)} %bitcast.2.base_ref, bf16[2,512,1024]{2,1,0:T(8,128)(2,1)} %copy.171.q_ref, bf16[2,1024,512]{2,1,0:T(8,128)(2,1)} %maximum_maximum_fusion.kv_ref), custom_call_target="tpu_custom_call" | custom-call | flops 4294967296 | bytes 8388608 | tf_op jit(solution)/shard_map/pallas_call | solution.py:126
  155.4 2.5 all-gather.7.cloned.1.call-done
  157.9 40.0 %shard_map.178 = (bf16[1024,640]{1,0:T(8,128)(2,1)}, f32[1024,640]{1,0:T(8,128)}, bf16[1024,1024]{1,0:T(8,128)(2,1)}, bf16[1024,2048]{1,0:T(8,128)(2,1)}, bf16[1...) custom-call(bf16[1024,640]{1,0:T(8,128)(2,1)} %bitcast.110, ...), custom_call_target="tpu_custom_call" | custom-call | flops 18790481920 | bytes 41943040 | tf_op jit(solution)/shard_map/pallas_call | solution.py:291
  198.0 15.1 %shard_map.179 = bf16[8,4,240,512]{3,2,1,0:T(8,128)(2,1)} custom-call(bf16[1024,640]{1,0:T(8,128)(2,1)} %get-tuple-element.30.ffw_in, bf16[1024,640]{1,0:T(8,128)(2,1)} %get-tuple-element.31.d_down, bf16[1024,2048]{1,0:T(8,128)(2,1)} %get-tuple-element.32.d_gate, bf16[1024,2048]{1,0:T(8,128)(2,1)} %get-tuple-element.33.d_up, ...), custom_call_target="tpu_custom_call" | custom-call | flops 8053063680 | bytes 25165824 | tf_op jit(solution)/shard_map/pallas_call | solution.py:329
  213.0 17.4 %shard_map.180 = (f32[2,512,1024]{2,1,0:T(8,128)}, f32[2,1024,512]{2,1,0:T(8,128)}) custom-call(s32[1]{0:T(128)} %bitcast.2.base_ref, bf16[2,512,1024]{2,1,0:T(8,128)(2,1)} %copy.171.q_ref, bf16[2,1024,512]{2,1,0:T(8,128)(2,1)} %maximum_maximum_fusion.kv_ref, bf16[2,512,1024]{2,1,0:T(8,128)(2,1)} %bitcast.136), custom_call_target="tpu_custom_call" | custom-call | flops 10737418240 | bytes 16777216 | tf_op jit(solution)/shard_map/pallas_call | solution.py:169
  230.5 2.8 slice.213
  234.5 5.6 %copy.174 = f32[2,512,1024]{1,2,0:T(8,128)} copy(f32[2,512,1024]{2,1,0:T(8,128)} %get-tuple-element.37) | data formatting | bytes 8388608 | tf_op jit(solution)/shard_map/reshape | solution.py:508
  240.1 3.1 multiply_subtract_fusion
  249.5 4.2 copy.151
  253.7 4.6 convolution_convert_fusion
  258.3 3.8 reshape.441
  262.1 4.3 copy.159
  266.4 3.9 fusion.42
  275.7 2.7 fusion.14
  281.4 2.0 fusion.3
  283.6 3.4 fusion.2
  287.6 60.7 %reduce-scatter.5.cloned.1.call-done = bf16[1,4,240,256]{2,3,1,0:T(8,128)(2,1)} async-done(((bf16[8,4,240,256]{2,3,1,0:T(8,128)(2,1)}), bf16[1,4,240,256]{2,3,1,0:T(8,128)(2,1)}) %reduce-scatter.5.cloned.1.call-update) | async-done | bytes 491536 | tf_op jit(solution)/shard_map/reduce_scatter | solution.py:378
  348.4 73.0 %reduce-scatter.9.cloned.1.call-done = bf16[1,4,240,512]{3,2,1,0:T(8,128)(2,1)} async-done(((bf16[8,4,240,512]{3,2,1,0:T(8,128)(2,1)}), bf16[1,4,240,512]{3,2,1,0:T(8,128)(2,1)}) %reduce-scatter.9.cloned.1.call-update) | async-done | bytes 983056 | tf_op jit(solution)/shard_map/reduce_scatter | solution.py:378
  421.4 4.3 fusion.13
  425.7 19.5 %reduce-scatter.7.cloned.1.call-done = bf16[1,240,256]{1,2,0:T(8,128)(2,1)} async-done(((bf16[4,240,256]{1,2,0:T(8,128)(2,1)}), bf16[1,240,256]{1,2,0:T(8,128)(2,1)}) %reduce-scatter.7.cloned.1.call-update) | async-done | bytes 122896 | tf_op jit(solution)/shard_map/reduce_scatter | solution.py:378
  449.0 22.8 %reduce-scatter.11.cloned.1.call-done = bf16[1,240,512]{2,1,0:T(8,128)(2,1)} async-done(((bf16[4,240,512]{2,1,0:T(8,128)(2,1)}), bf16[1,240,512]{2,1,0:T(8,128)(2,1)}) %reduce-scatter.11.cloned.1.call-update) | async-done | bytes 245776 | tf_op jit(solution)/shard_map/reduce_scatter | solution.py:378
  (157 shorter events, 58.9 us)
Async XLA Ops:
  7.2 74.3 %copy-start.2 = (bf16[2,512,640]{2,1,0:T(8,128)(2,1)S(1)}, bf16[2,512,640]{2,1,0:T(8,128)(2,1)}, u32[]{:S(2)}) copy-start(bf16[2,512,640]{2,1,0:T(8,128)(2,1)} %param.10) | copy-start | bytes 3932164
  7.2 68.9 %all-gather.5.cloned.1.call-start = ((), (), s32[]{:S(2)}) async-start(), calls=%async_computation.8 | async-start | bytes 4055040 | tf_op jit(solution)/shard_map/all_gather | solution.py:372
  12.1 145.8 %all-gather.7.cloned.1.call-start = ((), (), s32[]{:S(2)}) async-start(), calls=%async_computation.9 | async-start | bytes 8110080 | tf_op jit(solution)/shard_map/all_gather | solution.py:372
  76.2 272.1 %reduce-scatter.5.cloned.1.call-start = ((), (), s32[]{:S(2)}) async-start(), calls=%async_computation.4 | async-start | bytes 4718592 | tf_op jit(solution)/shard_map/reduce_scatter | solution.py:378
  78.1 6.4 %copy-start.7 = (f32[512,128]{1,0:T(8,128)}, f32[512,128]{1,0:T(8,128)S(1)}, u32[]{:S(2)}) copy-start(f32[512,128]{1,0:T(8,128)S(1)} %get-tuple-element.117) | copy-start | bytes 786436
  81.5 3.0 copy-start.5
  100.0 3.0 copy-start.9
  100.0 3.0 copy-start.10
  101.8 8.5 %copy-start.12 = (bf16[2,512,256]{2,1,0:T(8,128)(2,1)}, bf16[2,512,256]{2,1,0:T(8,128)(2,1)S(1)}, u32[]{:S(2)}) copy-start(bf16[2,512,256]{2,1,0:T(8,128)(2,1)S(1)} %convolution_convert_fusion.1) | copy-start | bytes 1572868
  103.0 41.3 %collective-permute-start = (bf16[2,512,512]{2,1,0:T(8,128)(2,1)}, bf16[2,512,512]{2,1,0:T(8,128)(2,1)}, u32[]{:S(2)}, u32[]{:S(2)}) collective-permute-start(bf16[2,512,512]{2,1,0:T(8,128)(2,1)} %pad_maximum_fusion.2), channel_id=1, source_target_pairs={{0,1},{1,2},{2,3},{4,5},{5,6},{6,7},{8,9},{9,10},{10,11},{12,13},{... | collective-permute-start | bytes 3145736 | tf_op jit(solution)/shard_map/ppermute | solution.py:25
  118.9 3.3 copy-start.20
  122.2 2.4 copy-start
  122.2 2.3 copy-start.17
  122.2 2.3 copy-start.18
  125.5 3.0 copy-start.22
  233.2 37.1 %collective-permute-start.1 = (bf16[2,512,512]{2,1,0:T(8,128)(2,1)}, bf16[2,512,512]{2,1,0:T(8,128)(2,1)}, u32[]{:S(2)}, u32[]{:S(2)}) collective-permute-start(bf16[2,512,512]{2,1,0:T(8,128)(2,1)} %slice.213), channel_id=1, source_target_pairs={{1,0},{2,1},{3,2},{5,4},{6,5},{7,6},{9,8},{10,9},{11,10},{13,12},{... | collective-permute-start | bytes 3145736 | tf_op jit(solution)/shard_map/ppermute | solution.py:25
  234.5 5.6 %copy-start.15 = (f32[512,128]{0,1:T(8,128)S(1)}, f32[512,128]{0,1:T(8,128)}, u32[]{:S(2)}) copy-start(f32[512,128]{0,1:T(8,128)} %copy.143) | copy-start | bytes 786436
  234.5 5.6 %copy-start.16 = (f32[512,128]{0,1:T(8,128)S(1)}, f32[512,128]{0,1:T(8,128)}, u32[]{:S(2)}) copy-start(f32[512,128]{0,1:T(8,128)} %copy.145) | copy-start | bytes 786436
  240.1 3.5 copy-start.1
  240.1 3.4 copy-start.21
  244.9 1.3 copy-start.3
  246.1 1.9 copy-start.11
  246.2 1.9 copy-start.19
  266.4 4.0 copy-start.6
  270.3 1.7 copy-start.8
  273.7 1.0 copy-start.14
  274.7 1.0 copy-start.13
  275.7 2.7 copy-start.23
  281.4 2.2 copy-start.4
  287.0 134.4 %reduce-scatter.9.cloned.1.call-start = ((), (), s32[]{:S(2)}) async-start(), calls=%async_computation.6 | async-start | bytes 8847360 | tf_op jit(solution)/shard_map/reduce_scatter | solution.py:378
  287.6 157.7 %reduce-scatter.7.cloned.1.call-start = ((), (), s32[]{:S(2)}) async-start(), calls=%async_computation.5 | async-start | bytes 655360 | tf_op jit(solution)/shard_map/reduce_scatter | solution.py:378
  348.3 123.5 %reduce-scatter.11.cloned.1.call-start = ((), (), s32[]{:S(2)}) async-start(), calls=%async_computation.7 | async-start | bytes 1228800 | tf_op jit(solution)/shard_map/reduce_scatter | solution.py:378
Sparse Core Ops, SparseCore 0:
  12.2 63.8 all-gather.4
  79.0 78.8 all-gather.6
  287.1 61.1 reduce-scatter.4
  352.0 69.3 reduce-scatter.8
  423.5 21.6 reduce-scatter.6
  447.4 24.3 reduce-scatter.10

commit v3 on v2

--- a/solution.py
+++ b/solution.py
@@ -304,7 +304,13 @@
     )(x, cot, mixed, gains_four, *weights)
 
 
-def sums_kernel(seqs, rows_a, rows_o, cols_f, ffw_in, d_down, d_gate, d_up, hidden, out):
+def out_rows(rows_o):
+    return -(-rows_o // 32) * 16
+
+
+def sums_kernel(
+    seqs, rows_a, rows_o, cols_f, ffw_in, d_down, d_attended, d_gate, d_up, hidden, mixed, out
+):
     at = pl.program_id(0)
     low = jnp.bfloat16
     each = d_gate.shape[1] // cols_f
@@ -316,27 +322,40 @@
                     s * rows_a : (s + 1) * rows_a, e * cols_f : (e + 1) * cols_f
                 ]
     total = dot(d_down[...], hidden[...], TN).astype(low)
+    total_out = dot(d_attended[...], mixed[...], TN).astype(low)
+    cols_o = total_out.shape[1]
+    upper, last = out_rows(rows_o), rows_a + rows_o
     for d in range(out.shape[0]):
-        out[d, at, rows_a:, :] = total[d * rows_o : (d + 1) * rows_o, :]
-
-
-def packed_sums(seqs, dps, sizes, ffw_in, d_down, d_gate, d_up, hidden):
-    rows_a, rows_o, cols_f, _, cols_d = sizes
+        out[d, at, rows_a:last, :] = total[d * rows_o : (d + 1) * rows_o, :]
+        out[d, at, last:, :cols_o] = total_out[d * rows_o : d * rows_o + upper, :]
+        out[d, at, last : last + rows_o - upper, cols_o:] = total_out[
+            d * rows_o + upper : (d + 1) * rows_o, :
+        ]
+        if rows_o < 2 * upper:
+            out[d, at, last + rows_o - upper :, cols_o:] = jnp.zeros(
+                (2 * upper - rows_o, cols_o), low
+            )
+
+
+def packed_sums(seqs, dps, sizes, ffw_in, d_down, d_attended, d_gate, d_up, hidden, mixed):
+    rows_a, rows_o, cols_f, cols_o, cols_d = sizes
     tokens = ffw_in.shape[0]
-    shape = (dps, seqs, rows_a + rows_o, cols_d)
+    shape = (dps, seqs, rows_a + rows_o + out_rows(rows_o), cols_d)
     whole = pl.BlockSpec((tokens, D), lambda i: (0, 0))
     part = pl.BlockSpec((tokens, cols_d), lambda i: (0, i))
     return pl.pallas_call(
         functools.partial(sums_kernel, seqs, rows_a, rows_o, cols_f),
         grid=(seqs,),
-        in_specs=[whole, whole, part, part, part],
+        in_specs=[whole] * 3
+        + [part] * 3
+        + [pl.BlockSpec((tokens, cols_o), lambda i: (0, i))],
         out_specs=pl.BlockSpec(shape, lambda i: (0, 0, 0, 0)),
         out_shape=jax.ShapeDtypeStruct(shape, jnp.bfloat16),
         compiler_params=pltpu.CompilerParams(vmem_limit_bytes=VMEM_BYTES),
         cost_estimate=pl.CostEstimate(
             flops=6 * tokens * D * cols_d * seqs, bytes_accessed=24 * 2**20, transcendentals=0
         ),
-    )(ffw_in, d_down, d_gate, d_up, hidden)
+    )(ffw_in, d_down, d_attended, d_gate, d_up, hidden, mixed)
 
 
 def rms_back(vector, scale_gain, gradient):
@@ -372,10 +391,6 @@
     return lax.all_gather(packed, ("seq", "dp")).reshape(
         (lax.axis_size("seq"), lax.axis_size("dp")) + packed.shape
     )
-
-
-def scatter(packed):
-    return lax.psum_scatter(lax.psum_scatter(packed, "dp"), "seq")
 
 
 def local(inputs, cotangent, w_query, w_key, w_value, w_out, w_gate, w_up, w_down, gains):
@@ -434,6 +449,7 @@
         and cols_f % 128 == 0
         and cols_o % 128 == 0
         and cols_d == 2 * cols_f
+        and cols_d == 2 * cols_o
         and dps == 2 * seqs
     )
     if aligned:
@@ -489,20 +505,27 @@
         )
 
     if aligned:
-        early = packed_sums(seqs, dps, sizes, ffw_in, d_down, d_gate, d_up, hidden)
+        early = packed_sums(
+            seqs, dps, sizes, ffw_in, d_down, d_attended, d_gate, d_up, hidden, mixed
+        )
     else:
         sum_gate = columns_parted(outer_sum(ffw_in, d_gate).astype(low), seqs, dps)
         sum_up = columns_parted(outer_sum(ffw_in, d_up).astype(low), seqs, dps)
         sum_down = rows_parted(outer_sum(d_down, hidden).astype(low), seqs, dps)
+        sum_out = rows_parted(outer_sum(d_attended, mixed).astype(low), seqs, dps)
+        upper = out_rows(rows_o)
+        wide = max(wide, 2 * cols_o)
+        halves = [sum_out[:, :, :upper], widened_four(sum_out[:, :, upper:], upper, cols_o)]
         early = jnp.concatenate(
             [
                 widened_four(jnp.concatenate([sum_gate, sum_up], axis=3), rows_a, wide),
                 widened_four(sum_down, rows_o, wide),
+                widened_four(jnp.concatenate(halves, axis=3), upper, wide),
             ],
             axis=2,
         )
     early, d_mixed = lax.optimization_barrier((early, d_mixed))
-    early = scatter(early)
+    early = lax.psum_scatter(early, "dp")
 
     d_queries, d_block = attend_back(base, queries, block, d_mixed)
     d_queries = d_queries.reshape(groups, stretch_len, HEADS, HD)
@@ -524,7 +547,6 @@
     sum_query = columns_parted(outer_sum(normed, d_q_lin).astype(low), seqs, dps)
     sum_key = columns_parted(outer_sum(normed, d_k_lin).astype(low), seqs, dps)
     sum_value = columns_parted(outer_sum(normed, d_values).astype(low), seqs, dps)
-    sum_out = rows_parted(outer_sum(d_attended, mixed).astype(low), seqs, dps)
     d_normed = (
         back_product(d_q_lin, full_query)
         + back_product(d_k_lin, full_key)
@@ -537,34 +559,46 @@
     ).reshape(full_gains.shape)
     sum_gains = columns_parted(sum_gains.astype(low), seqs, dps)
 
-    late = scatter(
+    narrow = -(-(lead + cols_g) // 128) * 128
+    late = widened_four(
         jnp.concatenate(
-            [
-                widened_four(
-                    jnp.concatenate(
-                        [sum_query, sum_key, sum_value, widened_four(sum_gains, rows_a, cols_g)],
-                        axis=3,
-                    ),
-                    rows_a,
-                    width,
-                ),
-                widened_four(sum_out, rows_o, width),
-            ],
-            axis=2,
-        )
-    )
-    early = early.astype(jnp.float32)
-    late = late.astype(jnp.float32)
+            [sum_query, sum_key, sum_value, widened_four(sum_gains, rows_a, cols_g)], axis=3
+        ),
+        rows_a,
+        narrow,
+    )
+    early, late = lax.optimization_barrier((early, late))
+    late = lax.psum_scatter(late, "dp")
+    middle_row = rows_a // 2
+    late = jnp.concatenate([late[:, :middle_row], late[:, middle_row:]], axis=2)
+    early_rows = early.shape[1]
+    broad = max(early.shape[2], 2 * narrow)
+    both = jnp.concatenate(
+        [
+            jnp.pad(part, ((0, 0), (0, 0), (0, broad - part.shape[2])))
+            for part in (early, late)
+        ],
+        axis=1,
+    )
+    both = lax.psum_scatter(both, "seq").astype(jnp.float32)
+    early = both[:early_rows]
+    late = jnp.concatenate(
+        [both[early_rows:, :narrow], both[early_rows:, narrow : 2 * narrow]], axis=0
+    )
+    last, upper = rows_a + rows_o, out_rows(rows_o)
+    grad_out = jnp.concatenate(
+        [early[last:, :cols_o], early[last : last + rows_o - upper, cols_o : 2 * cols_o]], axis=0
+    )
     return (
         outputs,
         grad_inputs,
         late[:rows_a, :cols_q],
         late[:rows_a, cols_q : cols_q + cols_k],
         late[:rows_a, cols_q + cols_k : lead],
-        late[rows_a:, : w_out.shape[0]].T,
+        grad_out.T,
         early[:rows_a, :cols_f],
         early[:rows_a, cols_f : 2 * cols_f],
-        early[rows_a:, : w_down.shape[0]].T,
+        early[rows_a:last, :cols_d].T,
         late[:rows_g, lead : lead + cols_g],
     )
 

time: 489 us -> 412 us (0.84)
  waiting for transfers between devices: 257 us -> 186 us
  matrix products: 21.9 us -> 14.8 us
    reduce_scatter x4 -> x3, waiting for transfers between devices: 176 us -> 81.9 us  [the longest x1 46.8 us: local(): late = lax.psum_scatter(late, 'dp')]
    ppermute x2, waiting for transfers between devices: 15.2 us -> 41.3 us  [shifted(): lax.ppermute(value, axis, [(source, source + steps) for source in range(f...]
    reshape x2 -> x0, local copies, waits for them, and re-layouts: 8.05 us -> none  [rows_parted(): whole.reshape(dps, rows // dps, seqs, cols // seqs).transpose(0, 2, 1, 3)]
    unnamed x64 -> x76, local copies, waits for them, and re-layouts: 12.3 us -> 11.6 us
  transfers between devices with their start and end apart: 8 -> 7, of which waited for: 7 -> 6; matrix products, arithmetic and copies ran while one was open for 20% -> 24% of each run, Pallas kernels for 2% -> 6%
where the time goes in v3:
time: 412 us; the launch traced here: 404 us
  waiting for transfers between devices  186 us (45%)
  Pallas kernels  83 us (20%)
  local copies, waits for them, and re-layouts  63.9 us (16%)
  other arithmetic  36.1 us (9%)
  between operations  14.9 us (4%)
  matrix products  14.8 us (4%)
  starting transfers between devices  5.71 us (1%)
    all_gather x2, waiting for transfers between devices, gather(): lax.all_gather(packed, ('seq', 'dp'))  62.3 us
    reduce_scatter x1, waiting for transfers between devices, local(): late = lax.psum_scatter(late, 'dp')  46.8 us
    ppermute x2, waiting for transfers between devices, shifted(): lax.ppermute(value, axis, [(source, source + steps) for source in range(f...  41.3 us
    pallas_call x1, Pallas kernels, middle_part(): pl.pallas_call(functools.partial(middle_kernel, sizes), grid=(tokens // s...  39.8 us
    reduce_scatter x1, waiting for transfers between devices, local(): both = lax.psum_scatter(both, 'seq').astype(jnp.float32)  30.1 us
    pallas_call x1, Pallas kernels, packed_sums(): pl.pallas_call(functools.partial(sums_kernel, seqs, rows_a, rows_o, cols_...  18 us
    pallas_call x1, Pallas kernels, attend_back(): pl.pallas_call(functools.partial(attend_back_kernel, step), grid=(groups,...  17.1 us
    unnamed x76, local copies, waits for them, and re-layouts  11.6 us
  transfers between devices with their start and end apart: 7, of which 6 were waited for; matrix products, arithmetic and copies ran while one was open for 24% of the time, Pallas kernels for 6%

profile of v3, /device:TPU:0, one launch (start us, length us, event | category | flops | bytes accessed | tf_op | source)
XLA Modules:
  0.0 404.0 jit_solution(5880990691753464413)
XLA Ops:
  13.8 62.3 %all-gather.5.cloned.1.call-done = bf16[7680,256]{1,0:T(8,128)(2,1)} async-done(((bf16[240,256]{1,0:T(8,128)(2,1)}), bf16[7680,256]{1,0:T(8,128)(2,1)}) %all-gather.5.cloned.1.call-update) | async-done | bytes 3932176 | tf_op jit(solution)/shard_map/all_gather | solution.py:391
  76.2 2.9 fusion.20
  81.2 2.5 slice.152.refs_0_
  88.2 2.4 copy.126
  93.1 3.9 slice_bitcast_fusion.1
  97.0 1.8 copy.134
  100.0 1.8 copy.131
  102.2 2.3 multiply_reduce_fusion.5
  111.4 4.2 %collective-permute-start = (bf16[2,512,512]{2,1,0:T(8,128)(2,1)}, bf16[2,512,512]{2,1,0:T(8,128)(2,1)}, u32[]{:S(2)}, u32[]{:S(2)}) collective-permute-start(bf16[2,512,512]{2,1,0:T(8,128)(2,1)} %pad_maximum_fusion.2), channel_id=1, source_target_pairs={{0,1},{1,2},{2,3},{4,5},{5,6},{6,7},{8,9},{9,10},{10,11},{12,13},{... | collective-permute-start | bytes 3145736 | tf_op jit(solution)/shard_map/ppermute | solution.py:25
  115.6 2.0 multiply_reduce_fusion.2
  122.2 4.4 %copy.168.q_ref = bf16[2,512,1024]{2,1,0:T(8,128)(2,1)} copy(bf16[2,512,1024]{1,2,0:T(8,128)(2,1)} %bitcast.109) | data formatting | bytes 4194304 | tf_op jit(solution)/shard_map/convert_element_type | solution.py:476
  127.7 26.1 %collective-permute-done = bf16[2,512,512]{2,1,0:T(8,128)(2,1)} collective-permute-done((bf16[2,512,512]{2,1,0:T(8,128)(2,1)}, bf16[2,512,512]{2,1,0:T(8,128)(2,1)}, u32[]{:S(2)}, u32[]{:S(2)}) %collective-permute-start) | collective-permute-done | bytes 1048608 | tf_op jit(solution)/shard_map/ppermute | solution.py:25
  153.8 2.7 maximum_maximum_fusion.kv_ref
  156.5 8.1 %shard_map.177 = bf16[2,512,1024]{2,1,0:T(8,128)(2,1)} custom-call(s32[1]{0:T(128)} %bitcast.2.base_ref, bf16[2,512,1024]{2,1,0:T(8,128)(2,1)} %copy.168.q_ref, bf16[2,1024,512]{2,1,0:T(8,128)(2,1)} %maximum_maximum_fusion.kv_ref), custom_call_target="tpu_custom_call" | custom-call | flops 4294967296 | bytes 8388608 | tf_op jit(solution)/shard_map/pallas_call | solution.py:126
  164.6 39.8 %shard_map.178 = (bf16[1024,640]{1,0:T(8,128)(2,1)}, f32[1024,640]{1,0:T(8,128)}, bf16[1024,1024]{1,0:T(8,128)(2,1)}, bf16[1024,2048]{1,0:T(8,128)(2,1)}, bf16[1...) custom-call(bf16[1024,640]{1,0:T(8,128)(2,1)} %bitcast.107, ...), custom_call_target="tpu_custom_call" | custom-call | flops 18790481920 | bytes 41943040 | tf_op jit(solution)/shard_map/pallas_call | solution.py:291
  204.5 18.0 %shard_map.179 = bf16[8,4,288,512]{3,2,1,0:T(8,128)(2,1)} custom-call(bf16[1024,640]{1,0:T(8,128)(2,1)} %get-tuple-element.32.ffw_in, bf16[1024,640]{1,0:T(8,128)(2,1)} %get-tuple-element.33.d_down, bf16[1024,640]{1,0:T(8,128)(2,1)} %get-tuple-element.34.d_attended, bf16[1024,2048]{1,0:T(8,128)(2,1)} %get-tuple-element.35.d_gate, ...), custom_call_target="tpu_custom_call" | custom-call | flops 8053063680 | bytes 25165824 | tf_op jit(solution)/shard_map/pallas_call | solution.py:346
  222.6 1.9 copy.142
  229.8 17.1 %shard_map.180 = (f32[2,512,1024]{2,1,0:T(8,128)}, f32[2,1024,512]{2,1,0:T(8,128)}) custom-call(s32[1]{0:T(128)} %bitcast.2.base_ref, bf16[2,512,1024]{2,1,0:T(8,128)(2,1)} %copy.168.q_ref, bf16[2,1024,512]{2,1,0:T(8,128)(2,1)} %maximum_maximum_fusion.kv_ref, bf16[2,512,1024]{2,1,0:T(8,128)(2,1)} %bitcast.130), custom_call_target="tpu_custom_call" | custom-call | flops 10737418240 | bytes 16777216 | tf_op jit(solution)/shard_map/pallas_call | solution.py:169
  246.9 2.9 slice.253
  251.1 5.6 %copy.171 = f32[2,512,1024]{1,2,0:T(8,128)} copy(f32[2,512,1024]{2,1,0:T(8,128)} %get-tuple-element.40) | data formatting | bytes 8388608 | tf_op jit(solution)/shard_map/reshape | solution.py:531
  256.7 3.1 multiply_subtract_fusion
  262.9 1.8 fusion.14
  266.5 1.8 fusion.42
  268.4 15.2 %collective-permute-done.1 = bf16[2,512,512]{2,1,0:T(8,128)(2,1)S(1)} collective-permute-done((bf16[2,512,512]{2,1,0:T(8,128)(2,1)}, bf16[2,512,512]{2,1,0:T(8,128)(2,1)S(1)}, u32[]{:S(2)}, u32[]{:S(2)}) %collective-permute-start.1) | collective-permute-done | bytes 1048608 | tf_op jit(solution)/shard_map/ppermute | solution.py:25
  285.9 2.6 fusion.11
  290.1 2.3 fusion.18
  297.2 2.9 fusion.13
  300.2 2.1 pad.24
  302.3 5.0 %reduce-scatter.4.cloned.1.call-done = bf16[1,4,288,512]{3,2,1,0:T(8,128)(2,1)} async-done(((bf16[8,4,288,512]{3,2,1,0:T(8,128)(2,1)}), bf16[1,4,288,512]{3,2,1,0:T(8,128)(2,1)}) %reduce-scatter.4.cloned.1.call-update) | async-done | bytes 1179664 | tf_op jit(solution)/shard_map/reduce_scatter | solution.py:528
  307.4 46.8 %reduce-scatter.6.cloned.1.call-done = bf16[1,4,160,256]{3,2,1,0:T(8,128)(2,1)} async-done(((bf16[8,4,160,256]{3,2,1,0:T(8,128)(2,1)}), bf16[1,4,160,256]{3,2,1,0:T(8,128)(2,1)}) %reduce-scatter.6.cloned.1.call-update) | async-done | bytes 327696 | tf_op jit(solution)/shard_map/reduce_scatter | solution.py:571
  356.6 4.3 %fusion.10 = bf16[2,512,640]{2,1,0:T(8,128)(2,1)} fusion(f32[2,512,640]{2,1,0:T(8,128)} %bitcast.119, bf16[2,512,640]{2,1,0:T(8,128)(2,1)S(1)} %copy-done.3, f32[2,512,640]{2,1,0:T(8,128)} %get-tuple-element.129, f32[2,512]{1,0:T(2,128)S(1)} %broadcast_multiply_fusion.2, f32[640]{0:T(1024)S(1)} %add.113, f32[2,512]{1,0:T(2,128)S(1)} %add_rsqrt_fusion.2), kind=kLoop, calls=%fused_computation.19 | loop fusion | flops 5242880 | bytes 7875072 | tf_op jit(solution)/shard_map/convert_element_type | solution.py:556
  360.9 30.1 %reduce-scatter.8.cloned.1.call-done = bf16[1,368,512]{2,1,0:T(8,128)(2,1)} async-done(((bf16[4,368,512]{2,1,0:T(8,128)(2,1)}), bf16[1,368,512]{2,1,0:T(8,128)(2,1)}) %reduce-scatter.8.cloned.1.call-update) | async-done | bytes 376848 | tf_op jit(solution)/shard_map/reduce_scatter | solution.py:583
  (168 shorter events, 58.2 us)
Async XLA Ops:
  7.2 73.7 %copy-start.2 = (bf16[2,512,640]{2,1,0:T(8,128)(2,1)S(1)}, bf16[2,512,640]{2,1,0:T(8,128)(2,1)}, u32[]{:S(2)}) copy-start(bf16[2,512,640]{2,1,0:T(8,128)(2,1)} %param.10) | copy-start | bytes 3932164
  7.2 68.9 %all-gather.5.cloned.1.call-start = ((), (), s32[]{:S(2)}) async-start(), calls=%async_computation.6 | async-start | bytes 4055040 | tf_op jit(solution)/shard_map/all_gather | solution.py:391
  12.1 152.5 %all-gather.7.cloned.1.call-start = ((), (), s32[]{:S(2)}) async-start(), calls=%async_computation.7 | async-start | bytes 8110080 | tf_op jit(solution)/shard_map/all_gather | solution.py:391
  76.2 231.2 %reduce-scatter.4.cloned.1.call-start = ((), (), s32[]{:S(2)}) async-start(), calls=%async_computation.3 | async-start | bytes 10616832 | tf_op jit(solution)/shard_map/reduce_scatter | solution.py:528
  79.2 6.0 %copy-start.10 = (f32[512,128]{1,0:T(8,128)}, f32[512,128]{1,0:T(8,128)S(1)}, u32[]{:S(2)}) copy-start(f32[512,128]{1,0:T(8,128)S(1)} %get-tuple-element.122) | copy-start | bytes 786436
  79.2 6.0 %copy-start.11 = (f32[512,128]{1,0:T(8,128)}, f32[512,128]{1,0:T(8,128)S(1)}, u32[]{:S(2)}) copy-start(f32[512,128]{1,0:T(8,128)S(1)} %get-tuple-element.124) | copy-start | bytes 786436
  107.4 2.1 copy-start.27
  109.5 1.8 copy-start.12
  109.5 1.8 copy-start.14
  109.6 6.0 %copy-start.19 = (bf16[1024,640]{1,0:T(8,128)(2,1)S(1)}, bf16[1024,640]{1,0:T(8,128)(2,1)}, u32[]{:S(2)}) copy-start(bf16[1024,640]{1,0:T(8,128)(2,1)} %copy.126) | copy-start | bytes 3932164
  110.2 5.4 %copy-start.16 = (bf16[2,512,256]{2,1,0:T(8,128)(2,1)}, bf16[2,512,256]{2,1,0:T(8,128)(2,1)S(1)}, u32[]{:S(2)}) copy-start(bf16[2,512,256]{2,1,0:T(8,128)(2,1)S(1)} %convolution_convert_fusion) | copy-start | bytes 1572868
  111.4 42.4 %collective-permute-start = (bf16[2,512,512]{2,1,0:T(8,128)(2,1)}, bf16[2,512,512]{2,1,0:T(8,128)(2,1)}, u32[]{:S(2)}, u32[]{:S(2)}) collective-permute-start(bf16[2,512,512]{2,1,0:T(8,128)(2,1)} %pad_maximum_fusion.2), channel_id=1, source_target_pairs={{0,1},{1,2},{2,3},{4,5},{5,6},{6,7},{8,9},{9,10},{10,11},{12,13},{... | collective-permute-start | bytes 3145736 | tf_op jit(solution)/shard_map/ppermute | solution.py:25
  117.6 2.4 copy-start
  117.6 2.3 copy-start.25
  117.6 2.3 copy-start.26
  122.2 4.9 %copy-start.29 = (f32[1,640]{1,0:T(1,128)S(1)}, f32[1,640]{1,0:T(1,128)}, u32[]{:S(2)}) copy-start(f32[1,640]{1,0:T(1,128)} %stack.15) | copy-start | bytes 7684
  122.2 31.6 %copy-start.13 = (bf16[2,512,128]{2,1,0:T(8,128)(2,1)S(1)}, bf16[2,512,128]{2,1,0:T(8,128)(2,1)}, u32[]{:S(2)}) copy-start(bf16[2,512,128]{2,1,0:T(8,128)(2,1)} %copy-done.12) | copy-start | bytes 786436
  122.2 31.6 %copy-start.15 = (bf16[2,512,128]{2,1,0:T(8,128)(2,1)S(1)}, bf16[2,512,128]{2,1,0:T(8,128)(2,1)}, u32[]{:S(2)}) copy-start(bf16[2,512,128]{2,1,0:T(8,128)(2,1)} %copy-done.14) | copy-start | bytes 786436
  122.2 31.6 %copy-start.17 = (bf16[2,512,256]{2,1,0:T(8,128)(2,1)S(1)}, bf16[2,512,256]{2,1,0:T(8,128)(2,1)}, u32[]{:S(2)}) copy-start(bf16[2,512,256]{2,1,0:T(8,128)(2,1)} %copy-done.16) | copy-start | bytes 1572868
  222.5 4.8 %copy-start.5 = (bf16[4,160,8,128]{3,2,1,0:T(8,128)(2,1)S(1)}, bf16[4,160,8,128]{3,2,1,0:T(8,128)(2,1)}, u32[]{:S(2)}) copy-start(bf16[4,160,8,128]{3,2,1,0:T(8,128)(2,1)} %copy-done.4) | copy-start | bytes 3932164
  222.5 131.7 %reduce-scatter.6.cloned.1.call-start = ((), (), s32[]{:S(2)}) async-start(), calls=%async_computation.4 | async-start | bytes 2949120 | tf_op jit(solution)/shard_map/reduce_scatter | solution.py:571
  249.8 33.8 %collective-permute-start.1 = (bf16[2,512,512]{2,1,0:T(8,128)(2,1)}, bf16[2,512,512]{2,1,0:T(8,128)(2,1)S(1)}, u32[]{:S(2)}, u32[]{:S(2)}) collective-permute-start(bf16[2,512,512]{2,1,0:T(8,128)(2,1)} %slice.253), channel_id=1, source_target_pairs={{1,0},{2,1},{3,2},{5,4},{6,5},{7,6},{9,8},{10,9},{11,10},{13,12},{... | collective-permute-start | bytes 3145736 | tf_op jit(solution)/shard_map/ppermute | solution.py:25
  251.0 5.6 %copy-start.23 = (f32[512,128]{0,1:T(8,128)S(1)}, f32[512,128]{0,1:T(8,128)}, u32[]{:S(2)}) copy-start(f32[512,128]{0,1:T(8,128)} %copy.142) | copy-start | bytes 786436
  251.1 5.6 %copy-start.24 = (f32[512,128]{0,1:T(8,128)S(1)}, f32[512,128]{0,1:T(8,128)}, u32[]{:S(2)}) copy-start(f32[512,128]{0,1:T(8,128)} %copy.140) | copy-start | bytes 786436
  256.7 3.6 copy-start.1
  264.8 1.7 copy-start.20
  266.5 17.1 %copy-start.7 = (f32[2,1024,512]{2,1,0:T(8,128)S(1)}, f32[2,1024,512]{2,1,0:T(8,128)}, u32[]{:S(2)}) copy-start(f32[2,1024,512]{2,1,0:T(8,128)} %get-tuple-element.41) | copy-start | bytes 12582916
  268.3 15.6 %copy-start.8 = (f32[512,128]{1,0:T(8,128)S(1)}, f32[512,128]{1,0:T(8,128)}, u32[]{:S(2)}) copy-start(f32[512,128]{1,0:T(8,128)} %get-tuple-element.121) | copy-start | bytes 786436
  268.4 15.6 %copy-start.9 = (f32[512,128]{1,0:T(8,128)S(1)}, f32[512,128]{1,0:T(8,128)}, u32[]{:S(2)}) copy-start(f32[512,128]{1,0:T(8,128)} %get-tuple-element.123) | copy-start | bytes 786436
  284.0 1.9 copy-start.6
  307.3 47.9 %copy-start.22 = (bf16[1,4,288,512]{3,2,1,0:T(8,128)(2,1)S(1)}, bf16[1,4,288,512]{3,2,1,0:T(8,128)(2,1)}, u32[]{:S(2)}) copy-start(bf16[1,4,288,512]{3,2,1,0:T(8,128)(2,1)} %reduce-scatter.4.cloned.1.call-done) | copy-start | bytes 3538948
  307.3 83.6 %reduce-scatter.8.cloned.1.call-start = ((), (), s32[]{:S(2)}) async-start(), calls=%async_computation.5 | async-start | bytes 1884160 | tf_op jit(solution)/shard_map/reduce_scatter | solution.py:583
  (5 other events, 6.2 us)
Sparse Core Ops, SparseCore 0:
  12.2 63.8 all-gather.4
  79.0 81.9 all-gather.6
  222.6 84.6 reduce-scatter.3
  310.5 43.6 reduce-scatter.5
  356.7 34.2 reduce-scatter.7
